TPU v7x, 512 devices: a whole 4x4x16 slice. The times are simulated.
512 devices in a mesh: wide: 64 (over z, x_hi, core), narrow: 8 (over y, x_lo).
Axes of the slice: x: 4 (x_hi: 2, x_lo: 2; x = x_hi * 2 + x_lo), y: 4, z: 16, core: 2. Of those that a mesh axis runs over, the one named last changes fastest.
Arguments:
- heat_power: float32 [8192, 8192], P('wide', 'narrow'), may hold values from 0 to 40, as said below
- level_taps: float32 [3, 17], replicated, may hold values from 0.02 to 0.1
- top_rows: float32 [1024, 1024], P('wide'), may hold values from 0 to 0.75
- top_cols: float32 [1024, 1024], P('narrow'), may hold values from 0 to 0.75
Outputs:
- temperature: float32 [8192, 8192], P('wide', 'narrow')
Inputs may be any that keep to these rules, and one draw needn't show every extreme that they name: `heat_power`: heater powers, not negative.
All inputs are finite; a program needn't handle non-finite values.
Results may differ from a plain program's by a relative error of at most 0.000053.
Values sent between devices are 32-bit elements; how exact they have to be, the bound alone decides.
A program may use at most 64 MiB of HBM per device.

v0:
```python
from functools import partial

import jax
import jax.numpy as jnp
from jax import lax
from jax.sharding import PartitionSpec as P


def padded_2(block, sides, width):
    for axis, dim in sides:
        count = lax.axis_size(axis)
        forward = [(i, i + 1) for i in range(count - 1)]
        backward = [(target, source) for source, target in forward]
        low = lax.ppermute(
            lax.slice_in_dim(block, block.shape[dim] - width, None, axis=dim), axis, forward
        )
        high = lax.ppermute(lax.slice_in_dim(block, 0, width, axis=dim), axis, backward)
        block = jnp.concatenate([low, block, high], axis=dim)
    return block


def stencil_along(padded, along, weights):
    count = weights.shape[0]
    length = padded.shape[along] - count + 1
    result = weights[0] * lax.slice_in_dim(padded, 0, length, axis=along)
    for offset in range(1, count):
        result = result + weights[offset] * lax.slice_in_dim(
            padded, offset, offset + length, axis=along
        )
    return result


def restrict_along(padded, along):
    length = padded.shape[along] - 2
    picks = [
        lax.slice_in_dim(padded, offset, offset + length - 1, stride=2, axis=along)
        for offset in range(4)
    ]
    return (picks[0] + picks[3]) * 0.125 + (picks[1] + picks[2]) * 0.375


def prolong_along(padded, along):
    length = padded.shape[along] - 2
    left_part = lax.slice_in_dim(padded, 0, length, axis=along)
    centre = lax.slice_in_dim(padded, 1, length + 1, axis=along)
    right_part = lax.slice_in_dim(padded, 2, length + 2, axis=along)
    even_cells = 0.75 * centre + 0.25 * left_part
    odd_cells = 0.75 * centre + 0.25 * right_part
    joined = jnp.stack([even_cells, odd_cells], along + 1)
    target = list(centre.shape)
    target[along] = 2 * length
    return joined.reshape(target)


def both_ways(field, margin, along_fn):
    padded = padded_2(field, (("wide", 0), ("narrow", 1)), margin)
    return along_fn(along_fn(padded, 0), 1)


def top_field(level_three, top_rows, top_cols):
    line_rows = lax.all_gather(level_three, "narrow", axis=1, tiled=True)
    whole_grid = lax.all_gather(line_rows, "wide", axis=0, tiled=True)
    row_summed = jnp.dot(top_rows, whole_grid, precision=lax.Precision.HIGHEST)
    return jnp.dot(row_summed, top_cols.T, precision=lax.Precision.HIGHEST)


def shards(heat_power, level_taps, top_rows, top_cols):
    margin = (level_taps.shape[1] - 1) // 2
    fields = [heat_power]
    for tier_index in range(3):
        fields.append(both_ways(fields[-1], 1, restrict_along))
    coarse = top_field(fields[3], top_rows, top_cols)
    for tier_index in (2, 1, 0):
        apply_taps = partial(stencil_along, weights=level_taps[tier_index])
        coarse = both_ways(fields[tier_index], margin, apply_taps) + both_ways(
            coarse, 1, prolong_along
        )
    return coarse


def solution(mesh):
    return jax.shard_map(
        shards,
        mesh=mesh,
        in_specs=(P("wide", "narrow"), P(), P("wide", None), P("narrow", None)),
        out_specs=P("wide", "narrow"),
        check_vma=False,
    )
```

profile of v0, /device:TPU:1, one launch (start us, length us, event | category | flops | bytes accessed | tf_op | source)
XLA Modules:
  0.0 400.2 jit_solution(11212421507627164920)
XLA Ops:
  6.5 0.8 fusion.125
  7.4 8.8 %collective-permute-start.5 = (f32[1,1024]{1,0:T(1,128)S(1)}, f32[1,1024]{1,0:T(1,128)S(1)}, u32[]{:S(2)}, u32[]{:S(2)}) collective-permute-start(f32[1,1024]{1,0:T(1,128)S(1)} %get-tuple-element.12), channel_id=1, source_target_pairs={{8,0},{16,8},{24,16},{32,24},{40,32},{48,40},{56,48},{64,56},{72,6... | collective-permute-start | bytes 12296 | tf_op jit(solution)/shard_map/ppermute | solution.py:17
  16.2 1.9 collective-permute-start.4
  18.1 1.1 collective-permute-done.4
  19.2 1.1 pad_maximum_fusion.1
  20.4 1.3 collective-permute-start.6
  21.7 1.3 collective-permute-start.7
  23.4 3.8 collective-permute-done.7
  28.4 4.5 %slice.915 = f32[64,512]{1,0:T(8,128)S(1)} slice(f32[64,1026]{1,0:T(8,128)S(1)} %multiply_add_fusion), slice={[0:64:1], [1:1024:2]} | slice | bytes 262144 | tf_op jit(solution)/shard_map/slice | solution.py:36
  32.9 4.5 %slice.916 = f32[64,512]{1,0:T(8,128)S(1)} slice(f32[64,1026]{1,0:T(8,128)S(1)} %multiply_add_fusion), slice={[0:64:1], [2:1025:2]} | slice | bytes 262144 | tf_op jit(solution)/shard_map/slice | solution.py:36
  37.4 4.5 %slice.913 = f32[64,512]{1,0:T(8,128)S(1)} slice(f32[64,1026]{1,0:T(8,128)S(1)} %multiply_add_fusion), slice={[0:64:1], [0:1023:2]} | slice | bytes 262144 | tf_op jit(solution)/shard_map/slice | solution.py:36
  41.9 4.5 %slice.914 = f32[64,512]{1,0:T(8,128)S(1)} slice(f32[64,1026]{1,0:T(8,128)S(1)} %multiply_add_fusion), slice={[0:64:1], [3:1026:2]} | slice | bytes 262144 | tf_op jit(solution)/shard_map/slice | solution.py:36
  46.4 2.9 collective-permute-start.13
  49.3 5.0 %collective-permute-start.12 = (f32[1,512]{1,0:T(1,128)S(1)}, f32[1,512]{1,0:T(1,128)S(1)}, u32[]{:S(2)}, u32[]{:S(2)}) collective-permute-start(f32[1,512]{1,0:T(1,128)S(1)} %get-tuple-element.27), channel_id=1, source_target_pairs={{0,8},{8,16},{16,24},{24,32},{32,40},{40,48},{48,56},{56,64},{64,7... | collective-permute-start | bytes 6152 | tf_op jit(solution)/shard_map/ppermute | solution.py:14
  55.1 1.3 collective-permute-start.15
  56.4 4.0 collective-permute-start.14
  60.4 1.0 collective-permute-done.14
  61.8 1.1 slice.982
  63.0 1.1 slice.983
  64.1 1.1 slice.980
  65.3 1.1 slice.981
  66.4 1.9 collective-permute-start.21
  68.4 6.8 %collective-permute-start.20 = (f32[1,256]{1,0:T(1,128)S(1)}, f32[1,256]{1,0:T(1,128)S(1)}, u32[]{:S(2)}, u32[]{:S(2)}) collective-permute-start(f32[1,256]{1,0:T(1,128)S(1)} %get-tuple-element.45), channel_id=1, source_target_pairs={{0,8},{8,16},{16,24},{24,32},{32,40},{40,48},{48,56},{56,64},{64,7... | collective-permute-start | bytes 3080 | tf_op jit(solution)/shard_map/ppermute | solution.py:14
  76.0 1.3 collective-permute-start.23
  77.3 4.4 %collective-permute-start.22 = (f32[34,1]{1,0:T(8,128)S(1)}, f32[34,1]{1,0:T(8,128)S(1)}, u32[]{:S(2)}, u32[]{:S(2)}) collective-permute-start(f32[34,1]{1,0:T(8,128)S(1)} %get-tuple-element.37), channel_id=1, source_target_pairs={{0,1},{1,2},{2,3},{3,4},{4,5},{5,6},{6,7},{8,9},{9,10},{10,11},{11... | collective-permute-start | bytes 416 | tf_op jit(solution)/shard_map/ppermute | solution.py:14
  81.7 0.9 collective-permute-done.22
  84.1 28.2 %all_gather.6 = f32[16,1024]{1,0:T(8,128)} all-gather(f32[16,128]{1,0:T(8,128)S(1)} %multiply_add_fusion.5), channel_id=1, replica_groups=mesh['wide'=64,'narrow'=8] {'narrow'}, dimensions={1}, use_global_device_ids=true | all-gather | bytes 73728 | tf_op jit(solution)/shard_map/all_gather | solution.py:61
  112.5 3.9 collective-permute-start.1
  116.5 1.0 copy.65
  117.5 10.8 %collective-permute-start = (f32[8,1024]{0,1:T(8,128)}, f32[8,1024]{0,1:T(8,128)S(1)}, u32[]{:S(2)}, u32[]{:S(2)}) collective-permute-start(f32[8,1024]{0,1:T(8,128)} %copy.65), channel_id=1, source_target_pairs={{0,8},{8,16},{16,24},{24,32},{32,40},{40,48},{48,56},{56,64},{64,7... | collective-permute-start | bytes 98312 | tf_op jit(solution)/shard_map/ppermute | solution.py:14
  129.8 1.9 collective-permute-start.17
  131.7 5.1 %collective-permute-start.16 = (f32[8,256]{1,0:T(8,128)S(1)}, f32[8,256]{1,0:T(8,128)S(1)}, u32[]{:S(2)}, u32[]{:S(2)}) collective-permute-start(f32[8,256]{1,0:T(8,128)S(1)} %get-tuple-element.41), channel_id=1, source_target_pairs={{0,8},{8,16},{16,24},{24,32},{32,40},{40,48},{48,56},{56,64},{64,7... | collective-permute-start | bytes 24584 | tf_op jit(solution)/shard_map/ppermute | solution.py:14
  137.7 2.7 collective-permute-done.16
  140.5 1.3 collective-permute-start.19
  141.8 4.0 collective-permute-start.18
  145.8 1.9 collective-permute-start.9
  147.8 6.4 %collective-permute-start.8 = (f32[8,512]{1,0:T(8,128)S(1)}, f32[8,512]{1,0:T(8,128)S(1)}, u32[]{:S(2)}, u32[]{:S(2)}) collective-permute-start(f32[8,512]{1,0:T(8,128)S(1)} %get-tuple-element.25), channel_id=1, source_target_pairs={{0,8},{8,16},{16,24},{24,32},{32,40},{40,48},{48,56},{56,64},{64,7... | collective-permute-start | bytes 49160 | tf_op jit(solution)/shard_map/ppermute | solution.py:14
  154.3 0.7 collective-permute-done.8
  155.1 1.3 collective-permute-start.11
  156.4 4.0 collective-permute-start.10
  160.4 10.6 %fusion.82 = f32[32,272]{1,0:T(8,128)S(1)} fusion(f32[48,272]{1,0:T(8,128)S(1)} %pad_maximum_fusion.9, f32[]{:T(128)} %bitcast.50, f32[]{:T(128)} %bitcast.49, f32[]{:T(128)} %bitcast.48, f32[]{:T(128)} %bitcast.47, f32[]{:T(128)} %bitcast.46, f32[]{:T(128)} %bitcast.45, f32[]{:T(128)} %bitcast.44, f32[]{:T(128)} %bitcast.43, f32[]{:T(128)} %bitcast.42, ...), kind=kLoop, calls=%fused_computation.178 | loop fusion | flops 287232 | bytes 626756 | tf_op jit(solution)/shard_map/add | solution.py:27
  171.2 110.6 %all-gather.2.cloned.1.call-done = f32[1024,1024]{1,0:T(8,128)} async-done(((f32[16,1024]{1,0:T(8,128)}), f32[1024,1024]{1,0:T(8,128)}) %all-gather.2.cloned.1.call-update) | async-done | bytes 4194320 | tf_op jit(solution)/shard_map/all_gather | solution.py:62
  281.8 4.4 %fusion.140 = f32[1024,16]{0,1:T(8,128)S(1)} fusion(f32[1024,1024]{1,0:T(8,128)} %all-gather.2.cloned.1.call-done, f32[16,1024]{1,0:T(8,128)S(1)} %copy-done.3), kind=kOutput, calls=%fused_computation.297 | convolution fusion | flops 201326592 | bytes 4325376 | tf_op jit(solution)/shard_map/dot_general | solution.py:63
  286.7 2.2 collective-permute-start.25
  288.9 4.9 %collective-permute-start.24 = (f32[1,128]{1,0:T(1,128)S(1)}, f32[1,128]{1,0:T(1,128)S(1)}, u32[]{:S(2)}, u32[]{:S(2)}) collective-permute-start(f32[1,128]{1,0:T(1,128)S(1)} %get-tuple-element.51), channel_id=1, source_target_pairs={{0,8},{8,16},{16,24},{24,32},{32,40},{40,48},{48,56},{56,64},{64,7... | collective-permute-start | bytes 1544 | tf_op jit(solution)/shard_map/ppermute | solution.py:14
  293.8 11.0 %fusion.41 = f32[64,528]{1,0:T(8,128)S(1)} fusion(f32[80,528]{1,0:T(8,128)S(1)} %pad_maximum_fusion.4, f32[]{:T(128)} %bitcast.33, f32[]{:T(128)} %bitcast.32, f32[]{:T(128)} %bitcast.31, f32[]{:T(128)} %bitcast.30, f32[]{:T(128)} %bitcast.29, f32[]{:T(128)} %bitcast.28, f32[]{:T(128)} %bitcast.27, f32[]{:T(128)} %bitcast.26, f32[]{:T(128)} %bitcast.25, ...), kind=kLoop, calls=%fused_computation.90 | loop fusion | flops 1115136 | bytes 2433092 | tf_op jit(solution)/shard_map/add | solution.py:27
  305.0 1.3 collective-permute-start.27
  306.3 4.0 collective-permute-start.26
  310.3 0.8 collective-permute-done.26
  311.5 10.7 %fusion.99 = f32[32,256]{1,0:T(8,128)S(1)} fusion(f32[32,256]{1,0:T(8,128)S(1)} %copy.70, f32[32,272]{1,0:T(8,128)S(1)} %fusion.82, f32[]{:T(128)} %bitcast.50, f32[]{:T(128)} %bitcast.49, f32[]{:T(128)} %bitcast.48, f32[]{:T(128)} %bitcast.47, f32[]{:T(128)} %bitcast.46, f32[]{:T(128)} %bitcast.45, f32[]{:T(128)} %bitcast.44, f32[]{:T(128)} %bitcast.43, ...), kind=kLoop, calls=%fused_computation.224 | loop fusion | flops 278528 | bytes 622660 | tf_op jit(solution)/shard_map/add | solution.py:75
  322.3 1.9 collective-permute-start.29
  324.2 5.1 %collective-permute-start.28 = (f32[1,256]{1,0:T(1,128)S(1)}, f32[1,256]{1,0:T(1,128)S(1)}, u32[]{:S(2)}, u32[]{:S(2)}) collective-permute-start(f32[1,256]{1,0:T(1,128)S(1)} %get-tuple-element.39), channel_id=1, source_target_pairs={{0,8},{8,16},{16,24},{24,32},{32,40},{40,48},{48,56},{56,64},{64,7... | collective-permute-start | bytes 3080 | tf_op jit(solution)/shard_map/ppermute | solution.py:14
  329.5 1.3 collective-permute-start.3
  330.9 1.3 collective-permute-start.31
  332.2 4.9 %collective-permute-start.30 = (f32[34,1]{1,0:T(8,128)S(1)}, f32[34,1]{1,0:T(8,128)S(1)}, u32[]{:S(2)}, u32[]{:S(2)}) collective-permute-start(f32[34,1]{1,0:T(8,128)S(1)} %get-tuple-element.35), channel_id=1, source_target_pairs={{0,1},{1,2},{2,3},{3,4},{4,5},{5,6},{6,7},{8,9},{9,10},{10,11},{11... | collective-permute-start | bytes 416 | tf_op jit(solution)/shard_map/ppermute | solution.py:14
  337.0 4.3 %collective-permute-start.2 = (f32[144,8]{0,1:T(8,128)S(1)}, f32[144,8]{0,1:T(8,128)S(1)}, u32[]{:S(2)}, u32[]{:S(2)}) collective-permute-start(f32[144,8]{0,1:T(8,128)S(1)} %get-tuple-element.5), channel_id=1, source_target_pairs={{0,1},{1,2},{2,3},{3,4},{4,5},{5,6},{6,7},{8,9},{9,10},{10,11},{11... | collective-permute-start | bytes 13832 | tf_op jit(solution)/shard_map/ppermute | solution.py:14
  342.0 11.4 %fusion.58 = f32[64,512]{1,0:T(8,128)S(1)} fusion(f32[64,512]{1,0:T(8,128)S(1)} %copy.73, f32[64,528]{1,0:T(8,128)S(1)} %fusion.41, f32[]{:T(128)} %bitcast.33, f32[]{:T(128)} %bitcast.32, f32[]{:T(128)} %bitcast.31, f32[]{:T(128)} %bitcast.30, f32[]{:T(128)} %bitcast.29, f32[]{:T(128)} %bitcast.28, f32[]{:T(128)} %bitcast.27, f32[]{:T(128)} %bitcast.26, ...), kind=kLoop, calls=%fused_computation.124 | loop fusion | flops 1114112 | bytes 2490436 | tf_op jit(solution)/shard_map/add | solution.py:75
  353.4 1.9 collective-permute-start.33
  355.3 5.8 %collective-permute-start.32 = (f32[1,512]{1,0:T(1,128)S(1)}, f32[1,512]{1,0:T(1,128)S(1)}, u32[]{:S(2)}, u32[]{:S(2)}) collective-permute-start(f32[1,512]{1,0:T(1,128)S(1)} %get-tuple-element.23), channel_id=1, source_target_pairs={{0,8},{8,16},{16,24},{24,32},{32,40},{40,48},{48,56},{56,64},{64,7... | collective-permute-start | bytes 6152 | tf_op jit(solution)/shard_map/ppermute | solution.py:14
  361.9 1.3 collective-permute-start.35
  363.2 4.0 collective-permute-start.34
  367.2 12.7 %fusion = f32[128,1040]{0,1:T(8,128)S(1)} fusion(f32[144,1040]{0,1:T(8,128)S(1)} %pad_maximum_fusion, f32[]{:T(128)} %bitcast.16, f32[]{:T(128)} %bitcast.15, f32[]{:T(128)} %bitcast.14, f32[]{:T(128)} %bitcast.13, f32[]{:T(128)} %bitcast.12, f32[]{:T(128)} %bitcast.11, f32[]{:T(128)} %bitcast.10, f32[]{:T(128)} %bitcast.9, f32[]{:T(128)} %bitcast.8, ...), kind=kLoop, calls=%fused_computation.3 | loop fusion | flops 4392960 | bytes 9584708 | tf_op jit(solution)/shard_map/add | solution.py:27
  381.2 11.2 %fusion.17 = f32[128,1024]{0,1:T(8,128)S(1)} fusion(f32[128,1024]{0,1:T(8,128)S(1)} %bitcast.82, f32[128,1040]{0,1:T(8,128)S(1)} %fusion, f32[]{:T(128)} %bitcast.16, f32[]{:T(128)} %bitcast.15, f32[]{:T(128)} %bitcast.14, f32[]{:T(128)} %bitcast.13, f32[]{:T(128)} %bitcast.12, f32[]{:T(128)} %bitcast.11, f32[]{:T(128)} %bitcast.10, f32[]{:T(128)} %bitcast.9, ...), kind=kLoop, calls=%fused_computation.37 | loop fusion | flops 4456448 | bytes 9961540 | tf_op jit(solution)/shard_map/add | solution.py:75
  392.4 1.0 copy.76
  (120 shorter events, 11.9 us)
Async XLA Ops:
  6.5 279.7 %copy-start = (f32[128,1024]{1,0:T(8,128)S(1)}, f32[128,1024]{1,0:T(8,128)}, u32[]{:S(2)}) copy-start(f32[128,1024]{1,0:T(8,128)} %param.7) | copy-start | bytes 1572868
  6.5 275.2 %all-gather.2.cloned.1.call-start = ((), (), s32[]{:S(2)}) async-start(), calls=%async_computation | async-start | bytes 4259840 | tf_op jit(solution)/shard_map/all_gather | solution.py:62
  7.4 10.7 %collective-permute-start.5 = (f32[1,1024]{1,0:T(1,128)S(1)}, f32[1,1024]{1,0:T(1,128)S(1)}, u32[]{:S(2)}, u32[]{:S(2)}) collective-permute-start(f32[1,1024]{1,0:T(1,128)S(1)} %get-tuple-element.12), channel_id=1, source_target_pairs={{8,0},{16,8},{24,16},{32,24},{40,32},{48,40},{56,48},{64,56},{72,6... | collective-permute-start | bytes 12296 | tf_op jit(solution)/shard_map/ppermute | solution.py:17
  16.2 3.1 collective-permute-start.4
  20.4 3.0 collective-permute-start.6
  21.7 5.5 %collective-permute-start.7 = (f32[130,1]{1,0:T(8,128)S(1)}, f32[130,1]{1,0:T(8,128)S(1)}, u32[]{:S(2)}, u32[]{:S(2)}) collective-permute-start(f32[130,1]{1,0:T(8,128)S(1)} %get-tuple-element.7), channel_id=1, source_target_pairs={{1,0},{2,1},{3,2},{4,3},{5,4},{6,5},{7,6},{9,8},{10,9},{11,10},{12... | collective-permute-start | bytes 1568 | tf_op jit(solution)/shard_map/ppermute | solution.py:17
  46.4 7.9 %collective-permute-start.13 = (f32[1,512]{1,0:T(1,128)S(1)}, f32[1,512]{1,0:T(1,128)S(1)}, u32[]{:S(2)}, u32[]{:S(2)}) collective-permute-start(f32[1,512]{1,0:T(1,128)S(1)} %get-tuple-element.28), channel_id=1, source_target_pairs={{8,0},{16,8},{24,16},{32,24},{40,32},{48,40},{56,48},{64,56},{72,6... | collective-permute-start | bytes 6152 | tf_op jit(solution)/shard_map/ppermute | solution.py:17
  49.3 5.7 %collective-permute-start.12 = (f32[1,512]{1,0:T(1,128)S(1)}, f32[1,512]{1,0:T(1,128)S(1)}, u32[]{:S(2)}, u32[]{:S(2)}) collective-permute-start(f32[1,512]{1,0:T(1,128)S(1)} %get-tuple-element.27), channel_id=1, source_target_pairs={{0,8},{8,16},{16,24},{24,32},{32,40},{40,48},{48,56},{56,64},{64,7... | collective-permute-start | bytes 6152 | tf_op jit(solution)/shard_map/ppermute | solution.py:14
  55.1 5.3 %collective-permute-start.15 = (f32[66,1]{1,0:T(8,128)S(1)}, f32[66,1]{1,0:T(8,128)S(1)}, u32[]{:S(2)}, u32[]{:S(2)}) collective-permute-start(f32[66,1]{1,0:T(8,128)S(1)} %get-tuple-element.22), channel_id=1, source_target_pairs={{1,0},{2,1},{3,2},{4,3},{5,4},{6,5},{7,6},{9,8},{10,9},{11,10},{12... | collective-permute-start | bytes 800 | tf_op jit(solution)/shard_map/ppermute | solution.py:17
  56.4 5.0 %collective-permute-start.14 = (f32[66,1]{1,0:T(8,128)S(1)}, f32[66,1]{1,0:T(8,128)S(1)}, u32[]{:S(2)}, u32[]{:S(2)}) collective-permute-start(f32[66,1]{1,0:T(8,128)S(1)} %get-tuple-element.21), channel_id=1, source_target_pairs={{0,1},{1,2},{2,3},{3,4},{4,5},{5,6},{6,7},{8,9},{9,10},{10,11},{11... | collective-permute-start | bytes 800 | tf_op jit(solution)/shard_map/ppermute | solution.py:14
  61.7 50.7 %copy-start.1 = (f32[128,1024]{1,0:T(8,128)S(1)}, f32[128,1024]{1,0:T(8,128)}, u32[]{:S(2)}) copy-start(f32[128,1024]{1,0:T(8,128)} %param.4) | copy-start | bytes 1572868
  66.4 61.9 %copy-start.2 = (f32[3,17]{1,0:T(4,128)S(1)}, f32[3,17]{1,0:T(4,128)}, u32[]{:S(2)}) copy-start(f32[3,17]{1,0:T(4,128)} %param.5) | copy-start | bytes 616
  66.4 8.8 %collective-permute-start.21 = (f32[1,256]{1,0:T(1,128)S(1)}, f32[1,256]{1,0:T(1,128)S(1)}, u32[]{:S(2)}, u32[]{:S(2)}) collective-permute-start(f32[1,256]{1,0:T(1,128)S(1)} %get-tuple-element.46), channel_id=1, source_target_pairs={{8,0},{16,8},{24,16},{32,24},{40,32},{48,40},{56,48},{64,56},{72,6... | collective-permute-start | bytes 3080 | tf_op jit(solution)/shard_map/ppermute | solution.py:17
  68.4 7.5 %collective-permute-start.20 = (f32[1,256]{1,0:T(1,128)S(1)}, f32[1,256]{1,0:T(1,128)S(1)}, u32[]{:S(2)}, u32[]{:S(2)}) collective-permute-start(f32[1,256]{1,0:T(1,128)S(1)} %get-tuple-element.45), channel_id=1, source_target_pairs={{0,8},{8,16},{16,24},{24,32},{32,40},{40,48},{48,56},{56,64},{64,7... | collective-permute-start | bytes 3080 | tf_op jit(solution)/shard_map/ppermute | solution.py:14
  76.0 5.7 %collective-permute-start.23 = (f32[34,1]{1,0:T(8,128)S(1)}, f32[34,1]{1,0:T(8,128)S(1)}, u32[]{:S(2)}, u32[]{:S(2)}) collective-permute-start(f32[34,1]{1,0:T(8,128)S(1)} %get-tuple-element.38), channel_id=1, source_target_pairs={{1,0},{2,1},{3,2},{4,3},{5,4},{6,5},{7,6},{9,8},{10,9},{11,10},{12... | collective-permute-start | bytes 416 | tf_op jit(solution)/shard_map/ppermute | solution.py:17
  77.3 5.3 %collective-permute-start.22 = (f32[34,1]{1,0:T(8,128)S(1)}, f32[34,1]{1,0:T(8,128)S(1)}, u32[]{:S(2)}, u32[]{:S(2)}) collective-permute-start(f32[34,1]{1,0:T(8,128)S(1)} %get-tuple-element.37), channel_id=1, source_target_pairs={{0,1},{1,2},{2,3},{3,4},{4,5},{5,6},{6,7},{8,9},{9,10},{10,11},{11... | collective-permute-start | bytes 416 | tf_op jit(solution)/shard_map/ppermute | solution.py:14
  112.5 216.8 %collective-permute-start.1 = (f32[8,1024]{0,1:T(8,128)S(1)}, f32[8,1024]{0,1:T(8,128)S(1)}, u32[]{:S(2)}, u32[]{:S(2)}) collective-permute-start(f32[8,1024]{0,1:T(8,128)S(1)} %copy.66), channel_id=1, source_target_pairs={{8,0},{16,8},{24,16},{32,24},{40,32},{48,40},{56,48},{64,56},{72,6... | collective-permute-start | bytes 98312 | tf_op jit(solution)/shard_map/ppermute | solution.py:17
  117.5 211.9 %collective-permute-start = (f32[8,1024]{0,1:T(8,128)}, f32[8,1024]{0,1:T(8,128)S(1)}, u32[]{:S(2)}, u32[]{:S(2)}) collective-permute-start(f32[8,1024]{0,1:T(8,128)} %copy.65), channel_id=1, source_target_pairs={{0,8},{8,16},{16,24},{24,32},{32,40},{40,48},{48,56},{56,64},{64,7... | collective-permute-start | bytes 98312 | tf_op jit(solution)/shard_map/ppermute | solution.py:14
  129.8 8.0 %collective-permute-start.17 = (f32[8,256]{1,0:T(8,128)S(1)}, f32[8,256]{1,0:T(8,128)S(1)}, u32[]{:S(2)}, u32[]{:S(2)}) collective-permute-start(f32[8,256]{1,0:T(8,128)S(1)} %get-tuple-element.42), channel_id=1, source_target_pairs={{8,0},{16,8},{24,16},{32,24},{40,32},{48,40},{56,48},{64,56},{72,6... | collective-permute-start | bytes 24584 | tf_op jit(solution)/shard_map/ppermute | solution.py:17
  131.7 8.8 %collective-permute-start.16 = (f32[8,256]{1,0:T(8,128)S(1)}, f32[8,256]{1,0:T(8,128)S(1)}, u32[]{:S(2)}, u32[]{:S(2)}) collective-permute-start(f32[8,256]{1,0:T(8,128)S(1)} %get-tuple-element.41), channel_id=1, source_target_pairs={{0,8},{8,16},{16,24},{24,32},{32,40},{40,48},{48,56},{56,64},{64,7... | collective-permute-start | bytes 24584 | tf_op jit(solution)/shard_map/ppermute | solution.py:14
  137.7 144.0 %copy-start.3 = (f32[16,1024]{1,0:T(8,128)S(1)}, f32[16,1024]{1,0:T(8,128)}, u32[]{:S(2)}) copy-start(f32[16,1024]{1,0:T(8,128)} %param.6) | copy-start | bytes 196612
  140.5 7.2 %collective-permute-start.19 = (f32[48,8]{1,0:T(8,128)S(1)}, f32[48,8]{1,0:T(8,128)S(1)}, u32[]{:S(2)}, u32[]{:S(2)}) collective-permute-start(f32[48,8]{1,0:T(8,128)S(1)} %get-tuple-element.34), channel_id=1, source_target_pairs={{1,0},{2,1},{3,2},{4,3},{5,4},{6,5},{7,6},{9,8},{10,9},{11,10},{12... | collective-permute-start | bytes 4616 | tf_op jit(solution)/shard_map/ppermute | solution.py:17
  141.8 12.4 %collective-permute-start.18 = (f32[48,8]{1,0:T(8,128)S(1)}, f32[48,8]{1,0:T(8,128)S(1)}, u32[]{:S(2)}, u32[]{:S(2)}) collective-permute-start(f32[48,8]{1,0:T(8,128)S(1)} %get-tuple-element.33), channel_id=1, source_target_pairs={{0,1},{1,2},{2,3},{3,4},{4,5},{5,6},{6,7},{8,9},{9,10},{10,11},{11... | collective-permute-start | bytes 4616 | tf_op jit(solution)/shard_map/ppermute | solution.py:14
  145.8 8.5 %collective-permute-start.9 = (f32[8,512]{1,0:T(8,128)S(1)}, f32[8,512]{1,0:T(8,128)S(1)}, u32[]{:S(2)}, u32[]{:S(2)}) collective-permute-start(f32[8,512]{1,0:T(8,128)S(1)} %get-tuple-element.26), channel_id=1, source_target_pairs={{8,0},{16,8},{24,16},{32,24},{40,32},{48,40},{56,48},{64,56},{72,6... | collective-permute-start | bytes 49160 | tf_op jit(solution)/shard_map/ppermute | solution.py:17
  147.8 7.3 %collective-permute-start.8 = (f32[8,512]{1,0:T(8,128)S(1)}, f32[8,512]{1,0:T(8,128)S(1)}, u32[]{:S(2)}, u32[]{:S(2)}) collective-permute-start(f32[8,512]{1,0:T(8,128)S(1)} %get-tuple-element.25), channel_id=1, source_target_pairs={{0,8},{8,16},{16,24},{24,32},{32,40},{40,48},{48,56},{56,64},{64,7... | collective-permute-start | bytes 49160 | tf_op jit(solution)/shard_map/ppermute | solution.py:14
  155.1 15.9 %collective-permute-start.11 = (f32[80,8]{1,0:T(8,128)S(1)}, f32[80,8]{1,0:T(8,128)S(1)}, u32[]{:S(2)}, u32[]{:S(2)}) collective-permute-start(f32[80,8]{1,0:T(8,128)S(1)} %get-tuple-element.18), channel_id=1, source_target_pairs={{1,0},{2,1},{3,2},{4,3},{5,4},{6,5},{7,6},{9,8},{10,9},{11,10},{12... | collective-permute-start | bytes 7688 | tf_op jit(solution)/shard_map/ppermute | solution.py:17
  156.4 14.6 %collective-permute-start.10 = (f32[80,8]{1,0:T(8,128)S(1)}, f32[80,8]{1,0:T(8,128)S(1)}, u32[]{:S(2)}, u32[]{:S(2)}) collective-permute-start(f32[80,8]{1,0:T(8,128)S(1)} %get-tuple-element.17), channel_id=1, source_target_pairs={{0,1},{1,2},{2,3},{3,4},{4,5},{5,6},{6,7},{8,9},{9,10},{10,11},{11... | collective-permute-start | bytes 7688 | tf_op jit(solution)/shard_map/ppermute | solution.py:14
  286.7 18.1 %collective-permute-start.25 = (f32[1,128]{1,0:T(1,128)S(1)}, f32[1,128]{1,0:T(1,128)S(1)}, u32[]{:S(2)}, u32[]{:S(2)}) collective-permute-start(f32[1,128]{1,0:T(1,128)S(1)} %get-tuple-element.52), channel_id=1, source_target_pairs={{8,0},{16,8},{24,16},{32,24},{40,32},{48,40},{56,48},{64,56},{72,6... | collective-permute-start | bytes 1544 | tf_op jit(solution)/shard_map/ppermute | solution.py:17
  288.9 15.9 %collective-permute-start.24 = (f32[1,128]{1,0:T(1,128)S(1)}, f32[1,128]{1,0:T(1,128)S(1)}, u32[]{:S(2)}, u32[]{:S(2)}) collective-permute-start(f32[1,128]{1,0:T(1,128)S(1)} %get-tuple-element.51), channel_id=1, source_target_pairs={{0,8},{8,16},{16,24},{24,32},{32,40},{40,48},{48,56},{56,64},{64,7... | collective-permute-start | bytes 1544 | tf_op jit(solution)/shard_map/ppermute | solution.py:14
  305.0 5.3 %collective-permute-start.27 = (f32[18,1]{1,0:T(8,128)S(1)}, f32[18,1]{1,0:T(8,128)S(1)}, u32[]{:S(2)}, u32[]{:S(2)}) collective-permute-start(f32[18,1]{1,0:T(8,128)S(1)} %get-tuple-element.50), channel_id=1, source_target_pairs={{1,0},{2,1},{3,2},{4,3},{5,4},{6,5},{7,6},{9,8},{10,9},{11,10},{12... | collective-permute-start | bytes 224 | tf_op jit(solution)/shard_map/ppermute | solution.py:17
  306.3 4.8 %collective-permute-start.26 = (f32[18,1]{1,0:T(8,128)S(1)}, f32[18,1]{1,0:T(8,128)S(1)}, u32[]{:S(2)}, u32[]{:S(2)}) collective-permute-start(f32[18,1]{1,0:T(8,128)S(1)} %get-tuple-element.49), channel_id=1, source_target_pairs={{0,1},{1,2},{2,3},{3,4},{4,5},{5,6},{6,7},{8,9},{9,10},{10,11},{11... | collective-permute-start | bytes 224 | tf_op jit(solution)/shard_map/ppermute | solution.py:14
  322.3 8.5 %collective-permute-start.29 = (f32[1,256]{1,0:T(1,128)S(1)}, f32[1,256]{1,0:T(1,128)S(1)}, u32[]{:S(2)}, u32[]{:S(2)}) collective-permute-start(f32[1,256]{1,0:T(1,128)S(1)} %get-tuple-element.40), channel_id=1, source_target_pairs={{8,0},{16,8},{24,16},{32,24},{40,32},{48,40},{56,48},{64,56},{72,6... | collective-permute-start | bytes 3080 | tf_op jit(solution)/shard_map/ppermute | solution.py:17
  324.2 6.6 %collective-permute-start.28 = (f32[1,256]{1,0:T(1,128)S(1)}, f32[1,256]{1,0:T(1,128)S(1)}, u32[]{:S(2)}, u32[]{:S(2)}) collective-permute-start(f32[1,256]{1,0:T(1,128)S(1)} %get-tuple-element.39), channel_id=1, source_target_pairs={{0,8},{8,16},{16,24},{24,32},{32,40},{40,48},{48,56},{56,64},{64,7... | collective-permute-start | bytes 3080 | tf_op jit(solution)/shard_map/ppermute | solution.py:14
  329.5 31.7 %collective-permute-start.3 = (f32[144,8]{0,1:T(8,128)S(1)}, f32[144,8]{0,1:T(8,128)S(1)}, u32[]{:S(2)}, u32[]{:S(2)}) collective-permute-start(f32[144,8]{0,1:T(8,128)S(1)} %get-tuple-element.6), channel_id=1, source_target_pairs={{1,0},{2,1},{3,2},{4,3},{5,4},{6,5},{7,6},{9,8},{10,9},{11,10},{12... | collective-permute-start | bytes 13832 | tf_op jit(solution)/shard_map/ppermute | solution.py:17
  330.9 10.4 %collective-permute-start.31 = (f32[34,1]{1,0:T(8,128)S(1)}, f32[34,1]{1,0:T(8,128)S(1)}, u32[]{:S(2)}, u32[]{:S(2)}) collective-permute-start(f32[34,1]{1,0:T(8,128)S(1)} %get-tuple-element.36), channel_id=1, source_target_pairs={{1,0},{2,1},{3,2},{4,3},{5,4},{6,5},{7,6},{9,8},{10,9},{11,10},{12... | collective-permute-start | bytes 416 | tf_op jit(solution)/shard_map/ppermute | solution.py:17
  332.2 9.2 %collective-permute-start.30 = (f32[34,1]{1,0:T(8,128)S(1)}, f32[34,1]{1,0:T(8,128)S(1)}, u32[]{:S(2)}, u32[]{:S(2)}) collective-permute-start(f32[34,1]{1,0:T(8,128)S(1)} %get-tuple-element.35), channel_id=1, source_target_pairs={{0,1},{1,2},{2,3},{3,4},{4,5},{5,6},{6,7},{8,9},{9,10},{10,11},{11... | collective-permute-start | bytes 416 | tf_op jit(solution)/shard_map/ppermute | solution.py:14
  337.0 24.1 %collective-permute-start.2 = (f32[144,8]{0,1:T(8,128)S(1)}, f32[144,8]{0,1:T(8,128)S(1)}, u32[]{:S(2)}, u32[]{:S(2)}) collective-permute-start(f32[144,8]{0,1:T(8,128)S(1)} %get-tuple-element.5), channel_id=1, source_target_pairs={{0,1},{1,2},{2,3},{3,4},{4,5},{5,6},{6,7},{8,9},{9,10},{10,11},{11... | collective-permute-start | bytes 13832 | tf_op jit(solution)/shard_map/ppermute | solution.py:14
  353.4 8.2 %collective-permute-start.33 = (f32[1,512]{1,0:T(1,128)S(1)}, f32[1,512]{1,0:T(1,128)S(1)}, u32[]{:S(2)}, u32[]{:S(2)}) collective-permute-start(f32[1,512]{1,0:T(1,128)S(1)} %get-tuple-element.24), channel_id=1, source_target_pairs={{8,0},{16,8},{24,16},{32,24},{40,32},{48,40},{56,48},{64,56},{72,6... | collective-permute-start | bytes 6152 | tf_op jit(solution)/shard_map/ppermute | solution.py:17
  355.3 6.5 %collective-permute-start.32 = (f32[1,512]{1,0:T(1,128)S(1)}, f32[1,512]{1,0:T(1,128)S(1)}, u32[]{:S(2)}, u32[]{:S(2)}) collective-permute-start(f32[1,512]{1,0:T(1,128)S(1)} %get-tuple-element.23), channel_id=1, source_target_pairs={{0,8},{8,16},{16,24},{24,32},{32,40},{40,48},{48,56},{56,64},{64,7... | collective-permute-start | bytes 6152 | tf_op jit(solution)/shard_map/ppermute | solution.py:14
  361.9 18.0 %collective-permute-start.35 = (f32[66,1]{1,0:T(8,128)S(1)}, f32[66,1]{1,0:T(8,128)S(1)}, u32[]{:S(2)}, u32[]{:S(2)}) collective-permute-start(f32[66,1]{1,0:T(8,128)S(1)} %get-tuple-element.20), channel_id=1, source_target_pairs={{1,0},{2,1},{3,2},{4,3},{5,4},{6,5},{7,6},{9,8},{10,9},{11,10},{12... | collective-permute-start | bytes 800 | tf_op jit(solution)/shard_map/ppermute | solution.py:17
  363.2 16.7 %collective-permute-start.34 = (f32[66,1]{1,0:T(8,128)S(1)}, f32[66,1]{1,0:T(8,128)S(1)}, u32[]{:S(2)}, u32[]{:S(2)}) collective-permute-start(f32[66,1]{1,0:T(8,128)S(1)} %get-tuple-element.19), channel_id=1, source_target_pairs={{0,1},{1,2},{2,3},{3,4},{4,5},{5,6},{6,7},{8,9},{9,10},{10,11},{11... | collective-permute-start | bytes 800 | tf_op jit(solution)/shard_map/ppermute | solution.py:14
Sparse Core Ops, SparseCore 0:
  112.4 169.2 all-gather.1
where the time goes:
time: 408 us; the launch traced here: 400 us
  starting transfers between devices  126 us (31%)
  waiting for transfers between devices  124 us (30%)
  other arithmetic  71 us (17%)
  local copies, waits for them, and re-layouts  32.3 us (8%)
  blocking collectives  28.2 us (7%)
  between operations  14.4 us (4%)
  matrix products  4.94 us (1%)
    all_gather x1, waiting for transfers between devices, top_field(): whole_grid = lax.all_gather(line_rows, 'wide', axis=0, tiled=True)  111 us
    ppermute x18, starting transfers between devices, padded_2(): lax.ppermute(lax.slice_in_dim(block, block.shape[dim] - width, None, axis...  86.7 us
    ppermute x18, starting transfers between devices, padded_2(): lax.ppermute(lax.slice_in_dim(block, 0, width, axis=dim), axis, backward)  38.9 us
    add x3, other arithmetic, stencil_along(): result + weights[offset] * lax.slice_in_dim(padded, offset, offset + leng...  34.3 us
    add x3, other arithmetic, shards(): both_ways(fields[tier_index], margin, apply_taps)  33.3 us
    all_gather x1, blocking collectives, top_field(): line_rows = lax.all_gather(level_three, 'narrow', axis=1, tiled=True)  28.2 us
    slice x24, local copies, waits for them, and re-layouts, restrict_along(): lax.slice_in_dim(padded, offset, offset + length - 1, stride=2, axis=along)  24.8 us
    ppermute x18, waiting for transfers between devices, padded_2(): lax.ppermute(lax.slice_in_dim(block, block.shape[dim] - width, None, axis...  9.3 us
  transfers between devices with their start and end apart: 37, of which 12 were waited for; matrix products, arithmetic and copies ran while one was open for 17% of the time, Pallas kernels for 0%

commit v1 on v0

v1 whole, which is shorter than its diff:
```python
import functools

import jax
import jax.numpy as jnp
import ml_dtypes
import numpy as np
from jax import lax
from jax.experimental import pallas as pl
from jax.experimental.pallas import tpu as pltpu
from jax.sharding import PartitionSpec as P

F32 = jnp.float32
BF16 = jnp.bfloat16
MESH = pl.DeviceIdType.MESH
TAPS = 17
NZ, NQ, NN = 16, 4, 8
NW = NZ * NQ
ROWS, COLS = 128, 1024
HALO = 40
EXT = ROWS + 2 * HALO
SIDE = 128
WIDE = COLS + 2 * SIDE
TILE = 256
WIN = TILE + 2 * SIDE


def restriction(out_n, out_off, in_n, in_off, first, out_end, in_end):
    out_at = np.arange(out_n)[:, None] + out_off
    in_at = np.arange(in_n)[None, :] + in_off
    d = in_at - 2 * out_at
    m = np.where((d == 0) | (d == 1), 0.375, 0.0) + np.where((d == -1) | (d == 2), 0.125, 0.0)
    if first:
        m = np.where((out_at >= 0) & (in_at >= 0), m, 0.0)
    if out_end is not None:
        m = np.where((out_at < out_end) & (in_at < in_end), m, 0.0)
    return m


def prolongation(out_n, out_off, in_n, in_off, first, in_end):
    out_at = np.arange(out_n)[:, None] + out_off
    in_at = np.arange(in_n)[None, :] + in_off
    d = out_at - 2 * in_at
    m = np.where((d == 0) | (d == 1), 0.75, 0.0) + np.where((d == -1) | (d == 2), 0.25, 0.0)
    if first:
        m = np.where(in_at >= 0, m, 0.0)
    if in_end is not None:
        m = np.where(in_at < in_end, m, 0.0)
    return m


def level_maps(block, off, size, variant):
    first, last = variant == 0, variant == 2
    end = [block >> t if last else None for t in range(4)]
    r1 = restriction(size // 2, -off // 2, size, -off, first, end[1], end[0])
    r2 = restriction(size // 4, -off // 4, size // 2, -off // 2, first, end[2], end[1])
    r3 = restriction(block // 8, 0, size // 4, -off // 4, first, end[3], end[2])
    p1 = prolongation(block, 0, size // 2, -off // 2, first, end[1])
    p2 = prolongation(size // 2, -off // 2, size // 4, -off // 4, first, end[2])
    return r1, r2, r3, p1, p2


def top_prolong(block, in_n, in_off, variant):
    first, last = variant == 0, variant == 2
    end = [block >> t if last else None for t in range(4)]
    p3 = prolongation(block // 4 + 4, -2, in_n, in_off, first, end[3])
    p2 = prolongation(block // 2 + 4, -2, block // 4 + 4, -2, first, end[2])
    p1 = prolongation(block, 0, block // 2 + 4, -2, first, end[1])
    return p1 @ p2 @ p3


def padded(m, rows, cols):
    out = np.zeros((rows, cols))
    out[: m.shape[0], : m.shape[1]] = m
    return out


ROW_AT = dict(r3=(0, 16), r1=(16, 128), r21=(144, 64), p1=(208, 128), p12=(336, 128), top=(464, 128))
COL_AT = dict(r1=(0, 512), r21=(512, 512), p1=(1024, 256), p12=(1280, 128))


def constants():
    row_maps, col_maps, col_top, col_res = [], [], [], []
    for v in range(3):
        r1, r2, r3, p1, p2 = level_maps(ROWS, HALO, EXT, v)
        row_maps.append(
            np.concatenate(
                [
                    padded((r3 @ r2 @ r1)[:, HALO - 8 : HALO + ROWS + 8], 16, 256),
                    padded(r1, 128, 256),
                    padded(r2 @ r1, 64, 256),
                    padded(p1, 128, 256),
                    padded(p1 @ p2, 128, 256),
                    padded(top_prolong(ROWS, 24, -1, v), 128, 256),
                ]
            )
        )
        r1, r2, r3, p1, p2 = level_maps(TILE, SIDE, WIN, v)
        col_maps.append(
            np.concatenate(
                [r1.T, padded((r2 @ r1).T, 512, 256), p1.T, (p1 @ p2).T]
            )
        )
        r1, r2, r3, p1, p2 = level_maps(COLS, SIDE, WIDE, v)
        col_res.append((r3 @ r2 @ r1).T)
        col_top.append(top_prolong(COLS, 144, -8, v).T)
    as_bf16 = lambda ms: np.stack(ms).astype(ml_dtypes.bfloat16)
    return as_bf16(row_maps), as_bf16(col_maps), as_bf16(col_res), as_bf16(col_top)


def split(x):
    hi = x.astype(BF16)
    return hi, (x - hi.astype(F32)).astype(BF16)


def mm(a, b):
    return jnp.dot(a, b, preferred_element_type=F32)


def mm3(ah, al, bh, bl):
    return mm(ah, bh) + (mm(al, bh) + mm(ah, bl))


def mm_nt(a, b):
    return lax.dot_general(a, b, (((1,), (1,)), ((), ())), preferred_element_type=F32)


def band(shape, in_dim, shift, taps, level):
    d = (
        lax.broadcasted_iota(jnp.int32, shape, in_dim)
        - lax.broadcasted_iota(jnp.int32, shape, 1 - in_dim)
        + shift
    )
    out = jnp.zeros(shape, F32)
    for k in range(TAPS):
        out = jnp.where(d == k, taps[level, k], out)
    return out


def between(shape, dim, low, high):
    at = lax.broadcasted_iota(jnp.int32, shape, dim)
    return (at >= low) & (at < high)


def kernel(
    heat, taps, top_rows, top_cols, row_maps, col_maps, col_res, col_top, out,
    q, aa, at, ab, bx, rmap, cmap, cres, ctop,
    mr_h, mr_l, y_h, y_l, n_h, n_l, a_h, a_l,
    g, ps, pb, xb,
    load_sem, near_s, near_r, far_s, far_r, aa_s, aa_r, ah_s, ah_r, bx_s, bx_r,
    z1_s, z1_r, z2_s, z2_r, pb_s, pb_r, xb_s, xb_r,
):
    w, n = lax.axis_index("wide"), lax.axis_index("narrow")
    z, qi = w // NQ, w % NQ

    def dev(dw, dn):
        return ((w + dw + NW) % NW, (n + dn + NN) % NN)

    def in_z(dz):
        return (((z + dz + NZ) % NZ) * NQ + qi, n)

    def in_plane(k):
        return (z * NQ + (qi + k + NQ) % NQ, n)

    row_v = jnp.where(w == 0, 0, jnp.where(w == NW - 1, 2, 1))
    col_v = jnp.where(n == 0, 0, jnp.where(n == NN - 1, 2, 1))

    loads = [
        pltpu.make_async_copy(heat, q.at[HALO : HALO + ROWS, SIDE : SIDE + COLS], load_sem.at[0]),
        pltpu.make_async_copy(top_rows, aa.at[qi], load_sem.at[1]),
        pltpu.make_async_copy(top_cols, bx.at[8:136], load_sem.at[2]),
        pltpu.make_async_copy(row_maps.at[row_v], rmap, load_sem.at[3]),
        pltpu.make_async_copy(col_res.at[col_v], cres, load_sem.at[4]),
        pltpu.make_async_copy(col_maps.at[1], cmap.at[0], load_sem.at[5]),
        pltpu.make_async_copy(col_maps.at[col_v], cmap.at[1], load_sem.at[6]),
        pltpu.make_async_copy(col_top.at[col_v], ctop, load_sem.at[7]),
    ]
    for c in loads:
        c.start()

    barrier = pltpu.get_barrier_semaphore()
    turn = 2 - 4 * (z % 2)
    around = [(dw, dn) for dw in (-1, 0, 1) for dn in (-1, 0, 1) if (dw, dn) != (0, 0)]
    greet = [dev(dw, dn) for dw, dn in around]
    greet += [in_plane(-k) for k in (1, 2, 3)]
    greet += [dev(0, k) for k in (2, 3, 4, 5, 6)]
    greet += [in_z(-dz) for dz in (1, -1, 4, -4, 8)] + [in_z(-turn)]
    count = len(greet)
    greet += [(((z + NZ - 1) % NZ) * NQ + NQ - 1, n), (((z + 1) % NZ) * NQ, n)]
    for target in greet:
        pl.semaphore_signal(barrier, inc=1, device_id=target, device_id_type=MESH)
    pl.semaphore_wait(barrier, jnp.where((qi == 0) | (qi == NQ - 1), count + NQ, count))

    def send(src, dst, send_sem, recv_sem, target):
        c = pltpu.make_async_remote_copy(
            src_ref=src, dst_ref=dst, send_sem=send_sem, recv_sem=recv_sem,
            device_id=target, device_id_type=MESH,
        )
        c.start()
        return c

    near_rows = {1: (ROWS + HALO - 8, HALO - 8, 8), -1: (HALO, HALO + ROWS, 8)}
    far_rows = {1: (ROWS + HALO - 40, 0, 32), -1: (HALO + 8, HALO + ROWS + 8, 32)}
    same_rows = (HALO, HALO, ROWS)
    cols_of = {1: (COLS, 0, SIDE), -1: (SIDE, SIDE + COLS, SIDE), 0: (SIDE, SIDE, COLS)}

    def halo(rows, dw, dn, i, s_sem, r_sem):
        sr, tr, nr = rows
        sc, tc, nc = cols_of[dn]
        return send(
            q.at[sr : sr + nr, sc : sc + nc], q.at[tr : tr + nr, tc : tc + nc],
            s_sem.at[i], r_sem.at[i], dev(dw, dn),
        )

    loads[0].wait()
    near = [
        halo(near_rows[dw] if dw else same_rows, dw, dn, i, near_s, near_r)
        for i, (dw, dn) in enumerate(around)
    ]
    loads[1].wait()
    plane = [
        send(aa.at[qi], aa.at[qi], aa_s.at[k - 1], aa_r.at[k - 1], in_plane(k)) for k in (1, 2, 3)
    ]

    def rim_copy(src, dst, side, p, dz):
        return pltpu.make_async_remote_copy(
            src_ref=src, dst_ref=dst, send_sem=ah_s.at[p], recv_sem=ah_r.at[side],
            device_id=(((z + dz + NZ) % NZ) * NQ + p, n), device_id_type=MESH,
        )

    @pl.when(qi == NQ - 1)
    def _():
        for p in range(NQ):
            rim_copy(aa.at[NQ - 1, 8:16], at, 0, p, 1).start()

    @pl.when(qi == 0)
    def _():
        for p in range(NQ):
            rim_copy(aa.at[0, 0:8], ab, 1, p, -1).start()

    loads[2].wait()
    sides = [
        send(bx.at[128:136], bx.at[0:8], bx_s.at[0], bx_r.at[0], dev(0, 1)),
        send(bx.at[8:16], bx.at[136:144], bx_s.at[1], bx_r.at[1], dev(0, -1)),
    ]
    updown = [(dw, dn) for dw, dn in around if dw]
    far = [halo(far_rows[dw], dw, dn, i, far_s, far_r) for i, (dw, dn) in enumerate(updown)]

    loads[3].wait()

    def rm(name, cols):
        start, rows = ROW_AT[name]
        return rmap[start : start + rows, 0:cols]

    low, high = jnp.where(w == 0, HALO, 0), jnp.where(w == NW - 1, HALO + ROWS, EXT)
    t0 = jnp.where(
        between((ROWS, EXT), 1, low, high), band((ROWS, EXT), 1, 8 - HALO, taps, 0), 0.0
    )

    def row_level(level, size, res, pro):
        th, tl = split(band((size, size), 1, 8, taps, level))
        tr_h, tr_l = split(mm(th, res) + mm(tl, res))
        return mm(pro, tr_h) + mm(pro, tr_l)

    for i, m in enumerate(
        (t0, row_level(1, 128, rm("r1", EXT), rm("p1", 128)), row_level(2, 64, rm("r21", EXT), rm("p12", 64)))
    ):
        hi, lo = split(m)
        mr_h[i * ROWS : (i + 1) * ROWS, :] = hi
        mr_l[i * ROWS : (i + 1) * ROWS, :] = lo

    loads[4].wait()
    for c in near:
        c.wait_recv()
    q_hi, q_lo = split(q[HALO - 8 : HALO + ROWS + 8, :])
    r3 = rm("r3", ROWS + 16)
    by_rows_h, by_rows_l = split(mm(r3, q_hi) + mm(r3, q_lo))
    c3 = cres[...]
    slot, lane = z % 4, z // 4
    g[slot, lane] = mm(by_rows_h, c3) + mm(by_rows_l, c3)

    first_stage = [
        send(g.at[slot, lane], g.at[slot, lane], z1_s.at[i], z1_r.at[i], in_z(dz))
        for i, dz in enumerate((4, -4, 8))
    ]

    def col_maps_of(i, low, high):
        def cm(name, cols):
            start, rows = COL_AT[name]
            return cmap[i, start : start + rows, 0:cols]

        m = jnp.where(
            between((WIN, TILE), 0, low, high), band((WIN, TILE), 0, 8 - SIDE, taps, 0), 0.0
        )
        n_h[i, 0], n_l[i, 0] = split(m)
        for level, size, res, pro in (
            (1, 256, cm("r1", 256), cm("p1", 256)),
            (2, 128, cm("r21", 128), cm("p12", 256)),
        ):
            th, tl = split(band((size, size), 0, 8, taps, level))
            tp_h, tp_l = split(mm(th, pro) + mm(tl, pro))
            n_h[i, level], n_l[i, level] = split(mm(res, tp_h) + mm(res, tp_l))

    loads[5].wait()
    col_maps_of(0, 0, WIN)

    for c in first_stage:
        c.wait_recv()
    second_stage = [
        send(g.at[slot], g.at[slot], z2_s.at[i], z2_r.at[i], in_z(dz))
        for i, dz in enumerate((1, -1, turn))
    ]

    for c in plane:
        c.wait_recv()
    for side, dst in ((0, at), (1, ab)):
        rim_copy(dst, dst, side, 0, 1).wait_recv()
    m_at = lax.broadcasted_iota(jnp.int32, (COLS, 256), 1)
    wanted = 64 * (4 * ((m_at // 16) % 4) + m_at // 64) + 16 * qi + m_at % 16
    pick = jnp.where(lax.broadcasted_iota(jnp.int32, (COLS, 256), 0) == wanted, 1.0, 0.0).astype(BF16)
    top_h, top_l = split(
        jnp.concatenate([at[...], aa[0], aa[1], aa[2], aa[3], ab[...]], axis=0)
    )
    a_h[...] = mm(top_h, pick).astype(BF16)
    a_l[...] = mm(top_l, pick).astype(BF16)

    loads[6].wait()
    col_maps_of(
        1,
        jnp.where(n == 0, SIDE, 0),
        jnp.where(n == NN - 1, SIDE + TILE, WIN),
    )

    for c in second_stage:
        c.wait_recv()
    gathered = jnp.concatenate([g[r, s] for r in range(4) for s in range(4)], axis=0)
    g_h, g_l = split(gathered)
    ps[...] = mm3(a_h[...], a_l[...], g_h, g_l)
    partial_sums = []
    for k in (1, 2, 3):
        start = pl.multiple_of(16 * ((qi + k) % NQ), 16)
        partial_sums.append(
            send(ps.at[pl.ds(start, 32)], pb.at[k - 1], pb_s.at[k - 1], pb_r.at[k - 1], in_plane(k))
        )

    for c in far:
        c.wait_recv()
    for j in range(WIDE // 256):
        at_j = slice(256 * j, 256 * (j + 1))
        q_hi, q_lo = split(q[:, at_j])
        hi, lo = split(mm3(mr_h[...], mr_l[...], q_hi, q_lo))
        y_h[:, at_j] = hi
        y_l[:, at_j] = lo

    for c in partial_sums:
        c.wait_recv()
    own = pl.multiple_of(16 * qi, 16)
    total = (ps[pl.ds(own, 32), :] + pb[0]) + (pb[1] + pb[2])
    xb[n] = total[7:31, :]
    lines = [
        send(xb.at[n], xb.at[n], xb_s.at[k - 1], xb_r.at[k - 1], dev(0, k)) for k in range(1, NN)
    ]

    last = COLS // TILE - 1
    for j in range(last + 1):
        which = 0
        if j == 0:
            which = jnp.where(n == 0, 1, 0)
        if j == last:
            which = jnp.where(n == NN - 1, 1, 0)
        acc = None
        for t in range(3):
            rows = slice(t * ROWS, (t + 1) * ROWS)
            cols = slice(TILE * j, TILE * j + WIN)
            term = mm3(y_h[rows, cols], y_l[rows, cols], n_h[which, t], n_l[which, t])
            acc = term if acc is None else acc + term
        out[:, TILE * j : TILE * (j + 1)] = acc

    for c in sides:
        c.wait_recv()
    b_h, b_l = split(bx[...])
    loads[7].wait()

    for c in lines:
        c.wait_recv()
    x_h, x_l = split(jnp.concatenate([xb[i] for i in range(NN)], axis=1))
    e_h, e_l = split(mm_nt(x_h, b_h) + (mm_nt(x_l, b_h) + mm_nt(x_h, b_l)))
    up = ctop[...]
    f_h, f_l = split(mm(e_h, up) + mm(e_l, up))
    ur = rm("top", 24)
    out[...] += mm(ur, f_h) + mm(ur, f_l)

    for c in near + plane + sides + far + first_stage + second_stage + partial_sums + lines:
        c.wait_send()

    @pl.when(qi == NQ - 1)
    def _():
        for p in range(NQ):
            rim_copy(aa.at[NQ - 1, 8:16], at, 0, p, 1).wait_send()

    @pl.when(qi == 0)
    def _():
        for p in range(NQ):
            rim_copy(aa.at[0, 0:8], ab, 1, p, -1).wait_send()


def shards(maps, heat_power, level_taps, top_rows, top_cols):
    anywhere = pl.BlockSpec(memory_space=pl.ANY)
    dma = lambda k: pltpu.SemaphoreType.DMA((k,))
    sems = [8, 8, 8, 6, 6, 3, 3, 4, 2, 2, 2, 3, 3, 3, 3, 3, 3, 7, 7]
    return pl.pallas_call(
        kernel,
        out_shape=jax.ShapeDtypeStruct((ROWS, COLS), F32),
        in_specs=[anywhere, pl.BlockSpec(memory_space=pltpu.SMEM)] + [anywhere] * 6,
        out_specs=pl.BlockSpec(memory_space=pltpu.VMEM),
        scratch_shapes=[
            pltpu.VMEM((EXT, WIDE), F32),
            pltpu.VMEM((NQ, 16, COLS), F32),
            pltpu.VMEM((8, COLS), F32),
            pltpu.VMEM((8, COLS), F32),
            pltpu.VMEM((144, COLS), F32),
            pltpu.VMEM(maps[0].shape[1:], BF16),
            pltpu.VMEM((2,) + maps[1].shape[1:], BF16),
            pltpu.VMEM(maps[2].shape[1:], BF16),
            pltpu.VMEM(maps[3].shape[1:], BF16),
            pltpu.VMEM((3 * ROWS, EXT), BF16),
            pltpu.VMEM((3 * ROWS, EXT), BF16),
            pltpu.VMEM((3 * ROWS, WIDE), BF16),
            pltpu.VMEM((3 * ROWS, WIDE), BF16),
            pltpu.VMEM((2, 3, WIN, TILE), BF16),
            pltpu.VMEM((2, 3, WIN, TILE), BF16),
            pltpu.VMEM((80, 256), BF16),
            pltpu.VMEM((80, 256), BF16),
            pltpu.VMEM((4, 4, 16, 128), F32),
            pltpu.VMEM((80, 128), F32),
            pltpu.VMEM((3, 32, 128), F32),
            pltpu.VMEM((NN, 24, 128), F32),
        ]
        + [dma(k) for k in sems],
        compiler_params=pltpu.CompilerParams(
            collective_id=0, has_side_effects=True, vmem_limit_bytes=48 * 1024 * 1024
        ),
    )(heat_power, level_taps, top_rows, top_cols, *maps)


def solution(mesh):
    maps = constants()
    return jax.shard_map(
        functools.partial(shards, maps),
        mesh=mesh,
        in_specs=(P("wide", "narrow"), P(), P("wide", None), P("narrow", None)),
        out_specs=P("wide", "narrow"),
        check_vma=False,
    )
```

time: 408 us -> 55.9 us (0.14); the launches traced: 400 us -> 55.5 us
  starting transfers between devices: 126 us -> 0 us
  waiting for transfers between devices: 124 us -> 0 us
  other arithmetic: 71 us -> 0 us
  Pallas kernels: 0 us -> 47.5 us
  blocking collectives: 28.2 us -> 0 us
  local copies, waits for them, and re-layouts: 32.3 us -> 7.94 us
  between operations: 14.4 us -> 0.02 us
  matrix products: 4.94 us -> 0 us
    ppermute x36 -> x0, starting transfers between devices: 126 us -> none  [the longest x18 86.7 us: padded_2(): lax.ppermute(lax.slice_in_dim(block, block.shape[dim] - width, None, axis...]
    all_gather x1 -> x0, waiting for transfers between devices: 111 us -> none  [top_field(): whole_grid = lax.all_gather(line_rows, 'wide', axis=0, tiled=True)]
    add x12 -> x0, other arithmetic: 67.8 us -> none  [the longest x3 34.3 us: stencil_along(): result + weights[offset] * lax.slice_in_dim(padded, offset, offset + leng...]
    pallas_call x0 -> x1, Pallas kernels: none -> 47.5 us  [shards(): pl.pallas_call(kernel, out_shape=jax.ShapeDtypeStruct((ROWS, COLS), F32),...]
    slice x43 -> x0, local copies, waits for them, and re-layouts: 29.4 us -> none  [the longest x24 24.8 us: restrict_along(): lax.slice_in_dim(padded, offset, offset + length - 1, stride=2, axis=along)]
    all_gather x1 -> x0, blocking collectives: 28.2 us -> none  [top_field(): line_rows = lax.all_gather(level_three, 'narrow', axis=1, tiled=True)]
    ppermute x36 -> x0, waiting for transfers between devices: 13.1 us -> none  [the longest x18 9.3 us: padded_2(): lax.ppermute(lax.slice_in_dim(block, block.shape[dim] - width, None, axis...]
    unnamed x9 -> x15, local copies, waits for them, and re-layouts: 0.22 us -> 7.94 us
  transfers between devices with their start and end apart: 37 -> 0, of which waited for: 12 -> 0; matrix products, arithmetic and copies ran while one was open for 17% -> 0% of each run, Pallas kernels for 0% -> 0%
where the time goes in v1:
time: 55.9 us; the launch traced here: 55.5 us
  Pallas kernels  47.5 us (85%)
  local copies, waits for them, and re-layouts  7.94 us (14%)
    pallas_call x1, Pallas kernels, shards(): pl.pallas_call(kernel, out_shape=jax.ShapeDtypeStruct((ROWS, COLS), F32),...  47.5 us
    unnamed x15, local copies, waits for them, and re-layouts  7.94 us

profile of v1, /device:TPU:1, one launch (start us, length us, event | category | flops | bytes accessed | tf_op | source)
XLA Modules:
  0.0 55.5 jit_solution(14304339120364841801)
XLA Ops:
  0.0 0.0 copy-start
  0.0 1.2 %copy-done = bf16[3,1280,128]{2,1,0:T(8,128)(2,1)S(1)} copy-done((bf16[3,1280,128]{2,1,0:T(8,128)(2,1)S(1)}, bf16[3,1280,128]{2,1,0:T(8,128)(2,1)}, u32[]{:S(2)}) %copy-start) | copy-done | bytes 983064
  1.2 0.0 copy-start.1
  1.2 1.2 %copy-done.1 = bf16[3,592,256]{2,1,0:T(8,128)(2,1)S(1)} copy-done((bf16[3,592,256]{2,1,0:T(8,128)(2,1)S(1)}, bf16[3,592,256]{2,1,0:T(8,128)(2,1)}, u32[]{:S(2)}) %copy-start.1) | copy-done | bytes 909336
  2.4 0.0 copy-start.2
  2.4 1.2 %copy-done.2 = bf16[3,144,1024]{2,1,0:T(8,128)(2,1)S(1)} copy-done((bf16[3,144,1024]{2,1,0:T(8,128)(2,1)S(1)}, bf16[3,144,1024]{2,1,0:T(8,128)(2,1)}, u32[]{:S(2)}) %copy-start.2) | copy-done | bytes 884760
  3.5 0.0 copy-start.3
  3.5 1.0 %copy-done.3 = f32[128,1024]{1,0:T(8,128)S(1)} copy-done((f32[128,1024]{1,0:T(8,128)S(1)}, f32[128,1024]{1,0:T(8,128)}, u32[]{:S(2)}) %copy-start.3) | copy-done | bytes 524312
  4.6 0.0 copy-start.4
  4.6 1.0 %copy-done.4 = f32[128,1024]{1,0:T(8,128)S(1)} copy-done((f32[128,1024]{1,0:T(8,128)S(1)}, f32[128,1024]{1,0:T(8,128)}, u32[]{:S(2)}) %copy-start.4) | copy-done | bytes 524312
  5.6 0.0 copy-start.5
  5.6 0.8 %copy-done.5 = f32[16,1024]{1,0:T(8,128)S(1)} copy-done((f32[16,1024]{1,0:T(8,128)S(1)}, f32[16,1024]{1,0:T(8,128)}, u32[]{:S(2)}) %copy-start.5) | copy-done | bytes 65560
  6.5 0.0 copy-start.6
  6.5 0.7 %copy-done.6 = f32[3,17]{1,0:T(4,128)S(1)} copy-done((f32[3,17]{1,0:T(4,128)S(1)}, f32[3,17]{1,0:T(4,128)}, u32[]{:S(2)}) %copy-start.6) | copy-done | bytes 228
  7.2 47.5 %shard_map.82 = f32[128,1024]{1,0:T(8,128)S(1)} custom-call(f32[128,1024]{1,0:T(8,128)S(1)} %copy-done.3, f32[3,17]{1,0:T(4,128)S(1)} %copy-done.6, f32[16,1024]{1,0:T(8,128)S(1)} %copy-done.5, f32[128,1024]{1,0:T(8,128)S(1)} %copy-done.4, bf16[3,592,256]{2,1,0:T(8,128)(2,1)S(1)} %copy-done.1, bf16[3,1408,256]{2,1,0:T(8,128)(2,1)} %constant.9.clone.col_maps, ...), custom_call_target="tpu_custom_call" | custom-call | tf_op jit(solution)/shard_map/pallas_call | solution.py:410
  54.7 0.8 %copy.10 = f32[128,1024]{1,0:T(8,128)} copy(f32[128,1024]{1,0:T(8,128)S(1)} %shard_map.82) | data formatting | bytes 1048576
Async XLA Ops:
  0.0 1.2 %copy-start = (bf16[3,1280,128]{2,1,0:T(8,128)(2,1)S(1)}, bf16[3,1280,128]{2,1,0:T(8,128)(2,1)}, u32[]{:S(2)}) copy-start(bf16[3,1280,128]{2,1,0:T(8,128)(2,1)} %constant.10.clone.col_res) | copy-start | bytes 2949124
  1.2 1.2 %copy-start.1 = (bf16[3,592,256]{2,1,0:T(8,128)(2,1)S(1)}, bf16[3,592,256]{2,1,0:T(8,128)(2,1)}, u32[]{:S(2)}) copy-start(bf16[3,592,256]{2,1,0:T(8,128)(2,1)} %constant.8.clone.row_maps) | copy-start | bytes 2727940
  2.4 1.2 %copy-start.2 = (bf16[3,144,1024]{2,1,0:T(8,128)(2,1)S(1)}, bf16[3,144,1024]{2,1,0:T(8,128)(2,1)}, u32[]{:S(2)}) copy-start(bf16[3,144,1024]{2,1,0:T(8,128)(2,1)} %constant.11.clone.col_top) | copy-start | bytes 2654212
  3.5 1.0 %copy-start.3 = (f32[128,1024]{1,0:T(8,128)S(1)}, f32[128,1024]{1,0:T(8,128)}, u32[]{:S(2)}) copy-start(f32[128,1024]{1,0:T(8,128)} %heat.1) | copy-start | bytes 1572868
  4.6 1.0 %copy-start.4 = (f32[128,1024]{1,0:T(8,128)S(1)}, f32[128,1024]{1,0:T(8,128)}, u32[]{:S(2)}) copy-start(f32[128,1024]{1,0:T(8,128)} %top_cols.1) | copy-start | bytes 1572868
  5.6 0.8 %copy-start.5 = (f32[16,1024]{1,0:T(8,128)S(1)}, f32[16,1024]{1,0:T(8,128)}, u32[]{:S(2)}) copy-start(f32[16,1024]{1,0:T(8,128)} %top_rows.1) | copy-start | bytes 196612
  6.5 0.7 %copy-start.6 = (f32[3,17]{1,0:T(4,128)S(1)}, f32[3,17]{1,0:T(4,128)}, u32[]{:S(2)}) copy-start(f32[3,17]{1,0:T(4,128)} %taps.1) | copy-start | bytes 616

commit v2 on v1

v2 whole, which is shorter than its diff:
```python
import functools

import jax
import jax.numpy as jnp
import ml_dtypes
import numpy as np
from jax import lax
from jax.experimental import pallas as pl
from jax.experimental.pallas import tpu as pltpu
from jax.sharding import PartitionSpec as P

F32 = jnp.float32
BF16 = jnp.bfloat16
MESH = pl.DeviceIdType.MESH
TAPS = 17
NZ, NQ, NN, NY = 16, 4, 8, 4
NW = NZ * NQ
ROWS, COLS = 128, 1024
HALO = 40
EXT = ROWS + 2 * HALO
SIDE = 128
WIDE = COLS + 2 * SIDE
TILE = 128
MARGIN = 64
WIN = TILE + 2 * MARGIN
SPAN = COLS + 2 * MARGIN
TILES = COLS // TILE


def restriction(out_n, out_off, in_n, in_off, first, out_end, in_end):
    out_at = np.arange(out_n)[:, None] + out_off
    in_at = np.arange(in_n)[None, :] + in_off
    d = in_at - 2 * out_at
    m = np.where((d == 0) | (d == 1), 0.375, 0.0) + np.where((d == -1) | (d == 2), 0.125, 0.0)
    if first:
        m = np.where((out_at >= 0) & (in_at >= 0), m, 0.0)
    if out_end is not None:
        m = np.where((out_at < out_end) & (in_at < in_end), m, 0.0)
    return m


def prolongation(out_n, out_off, in_n, in_off, first, in_end):
    out_at = np.arange(out_n)[:, None] + out_off
    in_at = np.arange(in_n)[None, :] + in_off
    d = out_at - 2 * in_at
    m = np.where((d == 0) | (d == 1), 0.75, 0.0) + np.where((d == -1) | (d == 2), 0.25, 0.0)
    if first:
        m = np.where(in_at >= 0, m, 0.0)
    if in_end is not None:
        m = np.where(in_at < in_end, m, 0.0)
    return m


def level_maps(block, off, size, variant):
    first, last = variant == 0, variant == 2
    end = [block >> t if last else None for t in range(4)]
    r1 = restriction(size // 2, -off // 2, size, -off, first, end[1], end[0])
    r2 = restriction(size // 4, -off // 4, size // 2, -off // 2, first, end[2], end[1])
    p1 = prolongation(block, 0, size // 2, -off // 2, first, end[1])
    p2 = prolongation(size // 2, -off // 2, size // 4, -off // 4, first, end[2])
    return r1, r2, p1, p2


def top_prolong(block, in_n, in_off, variant):
    first, last = variant == 0, variant == 2
    end = [block >> t if last else None for t in range(4)]
    p3 = prolongation(block // 4 + 4, -2, in_n, in_off, first, end[3])
    p2 = prolongation(block // 2 + 4, -2, block // 4 + 4, -2, first, end[2])
    p1 = prolongation(block, 0, block // 2 + 4, -2, first, end[1])
    return p1 @ p2 @ p3


def own_to_top(block, variant):
    first, last = variant == 0, variant == 2
    end = [block >> t if last else None for t in range(4)]
    r1 = restriction(block // 2 + 16, -8, block, 0, first, end[1], end[0])
    r2 = restriction(block // 4 + 16, -8, block // 2 + 16, -8, first, end[2], end[1])
    r3 = restriction(block // 8 + 16, -8, block // 4 + 16, -8, first, end[3], end[2])
    return r3 @ r2 @ r1


def padded(m, rows, cols):
    out = np.zeros((rows, cols))
    out[: m.shape[0], : m.shape[1]] = m
    return out


ROW_AT = dict(r3=(0, 32), r1=(32, 128), r21=(160, 64), p1=(224, 128), p12=(352, 128), top=(480, 128))
COL_AT = dict(r1=(0, 256), r21=(256, 256), p1=(512, 128), p12=(640, 64))


def constants():
    row_maps, col_maps, col_top, col_res = [], [], [], []
    for v in range(3):
        r1, r2, p1, p2 = level_maps(ROWS, HALO, EXT, v)
        row_maps.append(
            np.concatenate(
                [
                    padded(own_to_top(ROWS, v), 32, 256),
                    padded(r1, 128, 256),
                    padded(r2 @ r1, 64, 256),
                    padded(p1, 128, 256),
                    padded(p1 @ p2, 128, 256),
                    padded(top_prolong(ROWS, 24, -1, v), 128, 256),
                ]
            )
        )
        r1, r2, p1, p2 = level_maps(TILE, MARGIN, WIN, v)
        col_maps.append(
            np.concatenate([r1.T, padded((r2 @ r1).T, 256, 128), p1.T, (p1 @ p2).T])
        )
        res = own_to_top(COLS, v)
        col_res.append(np.concatenate([res[8:136], res[136:144], np.zeros((112, COLS)), res[0:8]]).T)
        col_top.append(top_prolong(COLS, 144, -8, v).T)
    at = np.arange(512)
    sort = np.zeros((512, 512))
    sort[at, 128 * (at // 16 % 4) + 16 * (at // 64) + at % 16] = 1.0
    as_bf16 = lambda ms: np.stack(ms).astype(ml_dtypes.bfloat16)
    return as_bf16(row_maps), as_bf16(col_maps), as_bf16(col_res), as_bf16(col_top), as_bf16(sort)


def split(x):
    hi = x.astype(BF16)
    return hi, (x - hi.astype(F32)).astype(BF16)


def mm(a, b):
    return jnp.dot(a, b, preferred_element_type=F32)


def mm_right(a, b_h, b_l):
    return mm(jnp.concatenate([a, a], axis=1), jnp.concatenate([b_h, b_l], axis=0))


def mm_left(a_h, a_l, b):
    res = mm(jnp.concatenate([a_h, a_l], axis=0), b)
    return res[0 : a_h.shape[0]] + res[a_h.shape[0] :]


def mm_both(a_h, a_l, b_h, b_l):
    m, n = a_h.shape[0], b_h.shape[1]
    res = mm(jnp.concatenate([a_h, a_l], axis=0), jnp.concatenate([b_h, b_l], axis=1))
    return res[0:m, 0:n] + (res[0:m, n:] + res[m:, 0:n])


def mm_nt(a, b):
    return lax.dot_general(a, b, (((1,), (1,)), ((), ())), preferred_element_type=F32)


def band(shape, in_dim, shift, taps, level):
    chunks = []
    for start in range(0, shape[0], 64):
        part = (min(64, shape[0] - start), shape[1])
        row = lax.broadcasted_iota(jnp.int32, part, 0) + start
        col = lax.broadcasted_iota(jnp.int32, part, 1)
        d = (row - col if in_dim == 0 else col - row) + shift

        def place(k, m):
            return jnp.where(d == k, taps[level, k], m)

        chunks.append(lax.fori_loop(0, TAPS, place, jnp.zeros(part, F32)))
    return chunks[0] if len(chunks) == 1 else jnp.concatenate(chunks, axis=0)


def between(shape, dim, low, high):
    at = lax.broadcasted_iota(jnp.int32, shape, dim)
    return (at >= low) & (at < high)


def kernel(
    heat, taps_in, top_rows, top_cols, row_maps, col_maps, col_res, col_top, sort, out,
    taps, q, aw, to, ar, at, ab, bx, rmap, cmap, cres, ctop, perm,
    mr, y_hl, b_h, b_l, cm_w, es, nb, nb_mid, near_z, far_z, next_z, g, ps, pa, xb, acc,
    load_sem, rim_s, rim_r, halo_s, halo_r, aa_s, aa_r, ah_s, ah_r, bx_s, bx_r,
    z1_s, z1_r, z2_s, z2_r, pa_s, pa_r, xb_s, xb_r, out_s,
):
    w, n = lax.axis_index("wide"), lax.axis_index("narrow")
    z, qi = w // NQ, w % NQ
    y, xl = n // 2, n % 2

    def dev(dw, dn):
        return ((w + dw + NW) % NW, (n + dn + NN) % NN)

    def in_z(dz):
        return (((z + dz + NZ) % NZ) * NQ + qi, n)

    def in_row(k, dx):
        return (z * NQ + (qi + k + NQ) % NQ, 2 * y + (xl + dx) % 2)

    def in_y(dy):
        return (w, 2 * ((y + dy + NY) % NY) + xl)

    row_v = jnp.where(w == 0, 0, jnp.where(w == NW - 1, 2, 1))
    col_v = jnp.where(n == 0, 0, jnp.where(n == NN - 1, 2, 1))

    pairs = dict(
        heat=(heat, q.at[HALO : HALO + ROWS, SIDE : SIDE + COLS]),
        rows=(row_maps.at[row_v], rmap),
        res=(col_res.at[col_v], cres),
        top_rows=(top_rows, aw),
        sort=(sort, perm),
        top_cols=(top_cols, bx.at[8:136]),
        taps=(taps_in, taps),
        cols=(col_maps.at[1], cmap.at[0]),
        rim_cols=(col_maps.at[col_v], cmap.at[1]),
        top=(col_top.at[col_v], ctop),
    )
    loads = {
        name: pltpu.make_async_copy(src, dst, load_sem.at[i])
        for i, (name, (src, dst)) in enumerate(pairs.items())
    }
    for c in loads.values():
        c.start()

    barrier = pltpu.get_barrier_semaphore()
    around = [(dw, dn) for dw in (-1, 0, 1) for dn in (-1, 0, 1) if (dw, dn) != (0, 0)]
    greet = [dev(dw, dn) for dw, dn in around]
    hops = [(k, dx) for k in range(NQ) for dx in range(2) if (k, dx) != (0, 0)]
    greet += [in_row(-k, dx) for k, dx in hops]
    greet += [in_y(dy) for dy in (1, 2, 3)]
    greet += [in_z(dz) for dz in (1, -1, 3, -3, 6, -6, 8)]
    count = len(greet)
    greet += [(((z + NZ - 1) % NZ) * NQ + NQ - 1, n), (((z + 1) % NZ) * NQ, n)]
    for target in greet:
        pl.semaphore_signal(barrier, inc=1, device_id=target, device_id_type=MESH)

    def send(src, dst, send_sem, recv_sem, target):
        c = pltpu.make_async_remote_copy(
            src_ref=src, dst_ref=dst, send_sem=send_sem, recv_sem=recv_sem,
            device_id=target, device_id_type=MESH,
        )
        c.start()
        return c

    def rm(name, cols):
        start, rows = ROW_AT[name]
        return rmap[start : start + rows, 0:cols]

    own_rows = slice(HALO, HALO + ROWS)

    def strip(src, dst, i, target):
        return send(q.at[src], q.at[dst], halo_s.at[i], halo_r.at[i], target)

    loads["heat"].wait()
    loads["rows"].wait()
    loads["res"].wait()
    own_h, own_l = split(q[own_rows, SIDE : SIDE + COLS])
    r3 = rm("r3", ROWS)
    by_rows_h, by_rows_l = split(mm_right(r3, own_h, own_l))
    top = mm_left(by_rows_h, by_rows_l, cres[...])
    at_right = lax.broadcasted_iota(jnp.int32, (32, 128), 1) < 64
    es[:, 0:128] = jnp.where(at_right, 0.0, top[:, 128:256])
    es[:, 128:256] = top[:, 0:128]
    es[:, 256:384] = jnp.where(at_right, top[:, 128:256], 0.0)
    row_part = {-1: slice(0, 8), 0: slice(8, 24), 1: slice(24, 32)}
    col_part = {-1: slice(0, 128), 0: slice(128, 256), 1: slice(256, 384)}
    pl.semaphore_wait(barrier, jnp.where((qi == 0) | (qi == NQ - 1), count + NQ, count))
    rims = []
    for i, (dw, dn) in enumerate(around):
        dst = nb.at[i] if dw else nb_mid.at[i // 4]
        rims.append(
            send(es.at[row_part[dw], col_part[dn]], dst, rim_s.at[i], rim_r.at[i], dev(dw, dn))
        )

    strips = [
        strip((own_rows, slice(COLS, COLS + SIDE)), (own_rows, slice(0, SIDE)), 0, dev(0, 1)),
        strip((own_rows, slice(SIDE, 2 * SIDE)), (own_rows, slice(SIDE + COLS, WIDE)), 1, dev(0, -1)),
    ]

    loads["top_rows"].wait()
    loads["sort"].wait()
    halves = [split(aw[:, 512 * p : 512 * (p + 1)]) for p in range(2)]
    sorted_cols = mm(
        jnp.concatenate([halves[0][0], halves[1][0], halves[0][1], halves[1][1]], axis=0), perm[...]
    )
    sorted_cols = sorted_cols[0:32] + sorted_cols[32:64]
    for p in range(2):
        for k in range(NQ):
            to[k, p] = sorted_cols[16 * p : 16 * (p + 1), 128 * k : 128 * (k + 1)]
    plane = [
        send(to.at[(qi + k) % NQ], ar.at[qi], aa_s.at[k - 1], aa_r.at[k - 1], in_row(k, 0))
        for k in (1, 2, 3)
    ]
    ar[qi] = to[qi]

    def rim_copy(src, dst, side, p, dz):
        return pltpu.make_async_remote_copy(
            src_ref=src, dst_ref=dst, send_sem=ah_s.at[p], recv_sem=ah_r.at[side],
            device_id=(((z + dz + NZ) % NZ) * NQ + p, n), device_id_type=MESH,
        )

    def rim_down(p):
        return rim_copy(to.at[p, :, 8:16], at, 0, p, 1)

    def rim_up(p):
        return rim_copy(to.at[p, :, 0:8], ab, 1, p, -1)

    @pl.when(qi == NQ - 1)
    def _():
        for p in range(NQ):
            rim_down(p).start()

    @pl.when(qi == 0)
    def _():
        for p in range(NQ):
            rim_up(p).start()

    loads["top_cols"].wait()
    sides = [
        send(bx.at[128:136], bx.at[0:8], bx_s.at[0], bx_r.at[0], dev(0, 1)),
        send(bx.at[8:16], bx.at[136:144], bx_s.at[1], bx_r.at[1], dev(0, -1)),
    ]
    for c in rims:
        c.wait_recv()
    mid = nb_mid[0] + nb_mid[1]
    halves = [
        (es[8 + 8 * p : 16 + 8 * p, 128:256] + mid[8 * p : 8 * p + 8])
        + (nb[first] + (nb[first + 1] + nb[first + 2]))
        for p, first in ((0, 5), (1, 0))
    ]
    near_z[0] = jnp.concatenate(halves, axis=0)

    steps = (0, 3, -3, 6, -6)
    first_stage = [
        send(near_z.at[0], near_z.at[i], z1_s.at[i - 1], z1_r.at[i - 1], in_z(-steps[i]))
        for i in range(1, 5)
    ]
    first_stage.append(send(near_z.at[0], far_z, z1_s.at[4], z1_r.at[4], in_z(8)))

    for c in strips:
        c.wait_recv()
    outer = [
        strip(slice(ROWS, ROWS + HALO), slice(0, HALO), 2, dev(1, 0)),
        strip(slice(HALO, 2 * HALO), slice(HALO + ROWS, EXT), 3, dev(-1, 0)),
    ]

    loads["taps"].wait()

    low, high = jnp.where(w == 0, HALO, 0), jnp.where(w == NW - 1, HALO + ROWS, EXT)
    t0 = jnp.where(
        between((ROWS, EXT), 1, low, high), band((ROWS, EXT), 1, 8 - HALO, taps, 0), 0.0
    )

    def row_level(level, size, res, pro):
        th, tl = split(band((size, size), 1, 8, taps, level))
        tr_h, tr_l = split(mm_left(th, tl, res))
        return mm_right(pro, tr_h, tr_l)

    for i, m in enumerate(
        (t0, row_level(1, 128, rm("r1", EXT), rm("p1", 128)), row_level(2, 64, rm("r21", EXT), rm("p12", 64)))
    ):
        hi, lo = split(m)
        mr[i * ROWS : (i + 1) * ROWS, :] = hi
        mr[(i + 3) * ROWS : (i + 4) * ROWS, :] = lo

    def col_maps_of(i, low, high):
        def cm(name, cols):
            start, rows = COL_AT[name]
            return cmap[i, start : start + rows, 0:cols]

        maps = [
            jnp.where(
                between((WIN, TILE), 0, low, high),
                band((WIN, TILE), 0, 8 - MARGIN, taps, 0),
                0.0,
            )
        ]
        for level, size, res, pro in (
            (1, 128, cm("r1", 128), cm("p1", 128)),
            (2, 64, cm("r21", 64), cm("p12", 128)),
        ):
            th, tl = split(band((size, size), 0, 8, taps, level))
            tp_h, tp_l = split(mm_left(th, tl, pro))
            maps.append(mm_right(res, tp_h, tp_l))
        for t, m in enumerate(maps):
            hi, lo = split(m)
            cm_w[i, WIN * t : WIN * (t + 1), 0:TILE] = hi
            cm_w[i, WIN * t : WIN * (t + 1), TILE : 2 * TILE] = lo

    loads["cols"].wait()
    loads["rim_cols"].wait()

    @pl.loop(0, 2)
    def _(i):
        col_maps_of(
            i,
            jnp.where((i == 1) & (n == 0), MARGIN, 0),
            jnp.where((i == 1) & (n == NN - 1), MARGIN + TILE, WIN),
        )

    for c in plane:
        c.wait_recv()
    for side, dst in ((0, at), (1, ab)):
        rim_copy(dst, dst, side, 0, 1).wait_recv()
    blocks = [at] + [ar.at[k] for k in range(NQ)] + [ab]
    a_h, a_l = split(
        jnp.concatenate(
            [jnp.concatenate([b[0], b[1]], axis=1) for b in blocks], axis=0
        )
    )
    for c in sides:
        c.wait_recv()

    @pl.loop(0, COLS // 128)
    def _(j):
        at_j = pl.ds(pl.multiple_of(128 * j, 128), 128)
        b_h[:, at_j], b_l[:, at_j] = split(bx[:, at_j])

    loads["top"].wait()

    for c in first_stage[:4]:
        c.wait_recv()
    second_stage = [
        send(near_z, next_z.at[i], z2_s.at[i], z2_r.at[i], in_z(-dz)) for i, dz in enumerate((1, -1))
    ]
    for i, dz in enumerate(steps):
        g[(z + dz + NZ) % NZ] = near_z[i]
    first_stage[4].wait_recv()
    g[(z + 8) % NZ] = far_z[...]
    for k, on in enumerate((1, -1)):
        second_stage[k].wait_recv()
        for i, dz in enumerate(steps):
            g[(z + on + dz + NZ) % NZ] = next_z[k, i]
    g_h, g_l = split(g[...].reshape(256, 128))
    ps[...] = mm_both(a_h, a_l, g_h, g_l)

    partial_sums = []
    for i, (k, dx) in enumerate(hops):
        start = pl.multiple_of(16 * ((qi + k) % NQ), 16)
        partial_sums.append(
            send(ps.at[pl.ds(start, 32)], pa.at[xl, k], pa_s.at[i], pa_r.at[i], in_row(k, dx))
        )
    own = pl.multiple_of(16 * qi, 16)
    pa[xl, 0] = ps[pl.ds(own, 32), :]

    for c in outer:
        c.wait_recv()

    @pl.loop(0, SPAN // 128)
    def _(j):
        here = q[:, pl.ds(pl.multiple_of(128 * j, 128), 256)]
        hi, lo = split(pltpu.roll(here, 256 - MARGIN, 1)[:, 0:128])
        res = mm_both(mr[0 : 3 * ROWS], mr[3 * ROWS :], hi, lo)
        at_j = pl.ds(pl.multiple_of(128 * j, 128), 128)
        y_hl[0, :, at_j], y_hl[1, :, at_j] = split(res)

    for c in partial_sums:
        c.wait_recv()
    for b in range(2):
        total = (pa[b, 0] + pa[b, 1]) + (pa[b, 2] + pa[b, 3])
        xb[y, :, 128 * b : 128 * (b + 1)] = total[7:31, :]
    lines = [
        send(xb.at[y], xb.at[y], xb_s.at[k - 1], xb_r.at[k - 1], in_y(k)) for k in range(1, NY)
    ]

    @pl.loop(0, TILES)
    def _(j):
        at_rim = ((j == 0) & (n == 0)) | ((j == TILES - 1) & (n == NN - 1))
        at_j = pl.ds(pl.multiple_of(TILE * j, TILE), WIN)
        windows = [
            jnp.concatenate([y_hl[p, t * ROWS : (t + 1) * ROWS, at_j] for t in range(3)], axis=1)
            for p in range(2)
        ]
        both = mm(jnp.concatenate(windows, axis=0), cm_w[jnp.where(at_rim, 1, 0)])
        acc[:, pl.ds(pl.multiple_of(TILE * j, TILE), TILE)] = both[0:ROWS, 0:TILE] + (
            both[0:ROWS, TILE:] + both[ROWS:, 0:TILE]
        )

    for c in lines:
        c.wait_recv()
    lines_in = jnp.concatenate([xb[i] for i in range(NY)], axis=1)
    x_h, x_l = split(jnp.concatenate([lines_in, jnp.zeros((8, COLS), F32)], axis=0))
    with_hi = mm_nt(jnp.concatenate([x_h, x_l], axis=0), b_h[...])
    e_h, e_l = split(with_hi[0:32] + (with_hi[32:64] + mm_nt(x_h, b_l[...])))
    f_h, f_l = split(mm_left(e_h, e_l, ctop[...]))
    ur = rm("top", 32)
    pieces = []
    for i in range(4):
        at_i = slice(256 * i, 256 * (i + 1))
        acc[:, at_i] += mm_right(ur, f_h[:, at_i], f_l[:, at_i])
        pieces.append(pltpu.make_async_copy(acc.at[:, at_i], out.at[:, at_i], out_s.at[i]))
        pieces[-1].start()

    for c in rims + strips + plane + sides + outer + first_stage + second_stage + partial_sums + lines:
        c.wait_send()

    @pl.when(qi == NQ - 1)
    def _():
        for p in range(NQ):
            rim_down(p).wait_send()

    @pl.when(qi == 0)
    def _():
        for p in range(NQ):
            rim_up(p).wait_send()

    for c in pieces:
        c.wait()


def shards(maps, heat_power, level_taps, top_rows, top_cols):
    far_memory = pl.BlockSpec(memory_space=pltpu.HBM)
    sems = [10, 8, 8, 4, 4, 3, 3, 4, 2, 2, 2, 5, 5, 2, 2, 7, 7, 3, 3, 4]
    words = lambda *shape: pltpu.VMEM(shape, F32)
    halves = lambda *shape: pltpu.VMEM(shape, BF16)
    return pl.pallas_call(
        kernel,
        out_shape=jax.ShapeDtypeStruct((ROWS, COLS), F32),
        in_specs=[far_memory] * (4 + len(maps)),
        out_specs=far_memory,
        scratch_shapes=[
            pltpu.SMEM((3, TAPS), F32),
            words(EXT, WIDE),
            words(16, COLS),
            words(NQ, 2, 16, 128),
            words(NQ, 2, 16, 128),
            words(2, 8, 128),
            words(2, 8, 128),
            words(144, COLS),
            halves(*maps[0].shape[1:]),
            halves(2, *maps[1].shape[1:]),
            halves(*maps[2].shape[1:]),
            halves(*maps[3].shape[1:]),
            halves(*maps[4].shape),
            halves(6 * ROWS, EXT),
            halves(2, 3 * ROWS, SPAN),
            halves(144, COLS),
            halves(144, COLS),
            halves(2, 3 * WIN, 2 * TILE),
            words(32, 384),
            words(8, 8, 128),
            words(2, 16, 128),
            words(5, 16, 128),
            words(16, 128),
            words(2, 5, 16, 128),
            words(NZ, 16, 128),
            words(80, 128),
            words(2, NQ, 32, 128),
            words(NY, 24, 256),
            words(ROWS, COLS),
        ]
        + [pltpu.SemaphoreType.DMA((k,)) for k in sems],
        compiler_params=pltpu.CompilerParams(
            collective_id=0, has_side_effects=True, vmem_limit_bytes=62 * 1024 * 1024
        ),
    )(heat_power, level_taps, top_rows, top_cols, *maps)


def solution(mesh):
    maps = constants()
    return jax.shard_map(
        functools.partial(shards, maps),
        mesh=mesh,
        in_specs=(P("wide", "narrow"), P(), P("wide", None), P("narrow", None)),
        out_specs=P("wide", "narrow"),
        check_vma=False,
    )
```

time: 55.9 us -> 44.1 us (0.79)
  local copies, waits for them, and re-layouts: 7.94 us -> 1.89 us
  Pallas kernels: 47.5 us -> 42 us
    unnamed x15 -> x1, local copies, waits for them, and re-layouts: 7.94 us -> 1.89 us
    pallas_call x1, Pallas kernels: 47.5 us -> 42 us  [shards(): pl.pallas_call(kernel, out_shape=jax.ShapeDtypeStruct((ROWS, COLS), F32),...]
where the time goes in v2:
time: 44.1 us; the launch traced here: 43.9 us
  Pallas kernels  42 us (95%)
  local copies, waits for them, and re-layouts  1.89 us (4%)
    pallas_call x1, Pallas kernels, shards(): pl.pallas_call(kernel, out_shape=jax.ShapeDtypeStruct((ROWS, COLS), F32),...  42 us
    unnamed x1, local copies, waits for them, and re-layouts  1.89 us

profile of v2, /device:TPU:1, one launch (start us, length us, event | category | flops | bytes accessed | tf_op | source)
XLA Modules:
  0.0 43.9 jit_solution(15205338244212335815)
XLA Ops:
  0.0 42.0 %shard_map.91 = f32[128,1024]{1,0:T(8,128)} custom-call(f32[128,1024]{1,0:T(8,128)} %heat.1, f32[3,17]{1,0:T(4,128)} %taps_in.1, f32[16,1024]{1,0:T(8,128)} %top_rows.1, f32[128,1024]{1,0:T(8,128)} %top_cols.1, bf16[3,608,256]{2,1,0:T(8,128)(2,1)} %constant.10.clone.row_maps, bf16[3,704,128]{2,1,0:T(8,128)(2,1)} %constant.11.clone.col_maps, ...), custom_call_target="tpu_custom_call" | custom-call | tf_op jit(solution)/shard_map/pallas_call | solution.py:506
  42.0 1.9 %copy.11 = f32[128,1024]{1,0:T(8,128)} copy(f32[128,1024]{1,0:T(8,128)} %shard_map.91) | data formatting | bytes 1048576

commit v3 on v2

--- a/solution.py
+++ b/solution.py
@@ -170,9 +170,9 @@
 def kernel(
     heat, taps_in, top_rows, top_cols, row_maps, col_maps, col_res, col_top, sort, out,
     taps, q, aw, to, ar, at, ab, bx, rmap, cmap, cres, ctop, perm,
-    mr, y_hl, b_h, b_l, cm_w, es, nb, nb_mid, near_z, far_z, next_z, g, ps, pa, xb, acc,
+    mr, y_hl, b_h, b_l, cm_w, es, nb, nb_mid, g, ps, pa, xb, acc,
     load_sem, rim_s, rim_r, halo_s, halo_r, aa_s, aa_r, ah_s, ah_r, bx_s, bx_r,
-    z1_s, z1_r, z2_s, z2_r, pa_s, pa_r, xb_s, xb_r, out_s,
+    z_s, z_r, pa_s, pa_r, xb_s, xb_r, out_s,
 ):
     w, n = lax.axis_index("wide"), lax.axis_index("narrow")
     z, qi = w // NQ, w % NQ
@@ -209,8 +209,8 @@
         name: pltpu.make_async_copy(src, dst, load_sem.at[i])
         for i, (name, (src, dst)) in enumerate(pairs.items())
     }
-    for c in loads.values():
-        c.start()
+    for name in ("heat", "rows", "res"):
+        loads[name].start()
 
     barrier = pltpu.get_barrier_semaphore()
     around = [(dw, dn) for dw in (-1, 0, 1) for dn in (-1, 0, 1) if (dw, dn) != (0, 0)]
@@ -218,11 +218,14 @@
     hops = [(k, dx) for k in range(NQ) for dx in range(2) if (k, dx) != (0, 0)]
     greet += [in_row(-k, dx) for k, dx in hops]
     greet += [in_y(dy) for dy in (1, 2, 3)]
-    greet += [in_z(dz) for dz in (1, -1, 3, -3, 6, -6, 8)]
+    along = [8] + [d for dz in range(7, 0, -1) for d in (dz, -dz)]
+    greet += [in_z(dz) for dz in along]
     count = len(greet)
     greet += [(((z + NZ - 1) % NZ) * NQ + NQ - 1, n), (((z + 1) % NZ) * NQ, n)]
     for target in greet:
         pl.semaphore_signal(barrier, inc=1, device_id=target, device_id_type=MESH)
+    for name in ("top_rows", "sort", "top_cols", "taps", "cols", "rim_cols", "top"):
+        loads[name].start()
 
     def send(src, dst, send_sem, recv_sem, target):
         c = pltpu.make_async_remote_copy(
@@ -310,6 +313,13 @@
         send(bx.at[128:136], bx.at[0:8], bx_s.at[0], bx_r.at[0], dev(0, 1)),
         send(bx.at[8:16], bx.at[136:144], bx_s.at[1], bx_r.at[1], dev(0, -1)),
     ]
+    for c in strips:
+        c.wait_recv()
+    outer = [
+        strip(slice(ROWS, ROWS + HALO), slice(0, HALO), 2, dev(1, 0)),
+        strip(slice(HALO, 2 * HALO), slice(HALO + ROWS, EXT), 3, dev(-1, 0)),
+    ]
+
     for c in rims:
         c.wait_recv()
     mid = nb_mid[0] + nb_mid[1]
@@ -318,20 +328,10 @@
         + (nb[first] + (nb[first + 1] + nb[first + 2]))
         for p, first in ((0, 5), (1, 0))
     ]
-    near_z[0] = jnp.concatenate(halves, axis=0)
-
-    steps = (0, 3, -3, 6, -6)
-    first_stage = [
-        send(near_z.at[0], near_z.at[i], z1_s.at[i - 1], z1_r.at[i - 1], in_z(-steps[i]))
-        for i in range(1, 5)
-    ]
-    first_stage.append(send(near_z.at[0], far_z, z1_s.at[4], z1_r.at[4], in_z(8)))
-
-    for c in strips:
-        c.wait_recv()
-    outer = [
-        strip(slice(ROWS, ROWS + HALO), slice(0, HALO), 2, dev(1, 0)),
-        strip(slice(HALO, 2 * HALO), slice(HALO + ROWS, EXT), 3, dev(-1, 0)),
+    g[z] = jnp.concatenate(halves, axis=0)
+
+    column = [
+        send(g.at[z], g.at[z], z_s.at[i], z_r.at[i], in_z(dz)) for i, dz in enumerate(along)
     ]
 
     loads["taps"].wait()
@@ -408,19 +408,8 @@
 
     loads["top"].wait()
 
-    for c in first_stage[:4]:
-        c.wait_recv()
-    second_stage = [
-        send(near_z, next_z.at[i], z2_s.at[i], z2_r.at[i], in_z(-dz)) for i, dz in enumerate((1, -1))
-    ]
-    for i, dz in enumerate(steps):
-        g[(z + dz + NZ) % NZ] = near_z[i]
-    first_stage[4].wait_recv()
-    g[(z + 8) % NZ] = far_z[...]
-    for k, on in enumerate((1, -1)):
-        second_stage[k].wait_recv()
-        for i, dz in enumerate(steps):
-            g[(z + on + dz + NZ) % NZ] = next_z[k, i]
+    for c in column:
+        c.wait_recv()
     g_h, g_l = split(g[...].reshape(256, 128))
     ps[...] = mm_both(a_h, a_l, g_h, g_l)
 
@@ -481,7 +470,7 @@
         pieces.append(pltpu.make_async_copy(acc.at[:, at_i], out.at[:, at_i], out_s.at[i]))
         pieces[-1].start()
 
-    for c in rims + strips + plane + sides + outer + first_stage + second_stage + partial_sums + lines:
+    for c in rims + strips + plane + sides + outer + column + partial_sums + lines:
         c.wait_send()
 
     @pl.when(qi == NQ - 1)
@@ -500,7 +489,7 @@
 
 def shards(maps, heat_power, level_taps, top_rows, top_cols):
     far_memory = pl.BlockSpec(memory_space=pltpu.HBM)
-    sems = [10, 8, 8, 4, 4, 3, 3, 4, 2, 2, 2, 5, 5, 2, 2, 7, 7, 3, 3, 4]
+    sems = [10, 8, 8, 4, 4, 3, 3, 4, 2, 2, 2, 15, 15, 7, 7, 3, 3, 4]
     words = lambda *shape: pltpu.VMEM(shape, F32)
     halves = lambda *shape: pltpu.VMEM(shape, BF16)
     return pl.pallas_call(
@@ -530,9 +519,6 @@
             words(32, 384),
             words(8, 8, 128),
             words(2, 16, 128),
-            words(5, 16, 128),
-            words(16, 128),
-            words(2, 5, 16, 128),
             words(NZ, 16, 128),
             words(80, 128),
             words(2, NQ, 32, 128),

time: 44.1 us -> 43.7 us (level)
  no operation moved by 1% of the time
where the time goes in v3:
time: 43.7 us; the launch traced here: 43.5 us
  Pallas kernels  41.6 us (95%)
  local copies, waits for them, and re-layouts  1.89 us (4%)
    pallas_call x1, Pallas kernels, shards(): pl.pallas_call(kernel, out_shape=jax.ShapeDtypeStruct((ROWS, COLS), F32),...  41.6 us
    unnamed x1, local copies, waits for them, and re-layouts  1.89 us

profile of v3, /device:TPU:1, one launch (start us, length us, event | category | flops | bytes accessed | tf_op | source)
XLA Modules:
  0.0 43.5 jit_solution(2287030967052341998)
XLA Ops:
  0.0 41.6 %shard_map.91 = f32[128,1024]{1,0:T(8,128)} custom-call(f32[128,1024]{1,0:T(8,128)} %heat.1, f32[3,17]{1,0:T(4,128)} %taps_in.1, f32[16,1024]{1,0:T(8,128)} %top_rows.1, f32[128,1024]{1,0:T(8,128)} %top_cols.1, bf16[3,608,256]{2,1,0:T(8,128)(2,1)} %constant.10.clone.row_maps, bf16[3,704,128]{2,1,0:T(8,128)(2,1)} %constant.11.clone.col_maps, ...), custom_call_target="tpu_custom_call" | custom-call | tf_op jit(solution)/shard_map/pallas_call | solution.py:495
  41.6 1.9 %copy.11 = f32[128,1024]{1,0:T(8,128)} copy(f32[128,1024]{1,0:T(8,128)} %shard_map.91) | data formatting | bytes 1048576

commit v4 on v3

--- a/solution.py
+++ b/solution.py
@@ -18,6 +18,7 @@
 ROWS, COLS = 128, 1024
 HALO = 40
 EXT = ROWS + 2 * HALO
+DEEP = 256
 SIDE = 128
 WIDE = COLS + 2 * SIDE
 TILE = 128
@@ -148,18 +149,14 @@
 
 
 def band(shape, in_dim, shift, taps, level):
-    chunks = []
-    for start in range(0, shape[0], 64):
-        part = (min(64, shape[0] - start), shape[1])
-        row = lax.broadcasted_iota(jnp.int32, part, 0) + start
-        col = lax.broadcasted_iota(jnp.int32, part, 1)
-        d = (row - col if in_dim == 0 else col - row) + shift
-
-        def place(k, m):
-            return jnp.where(d == k, taps[level, k], m)
-
-        chunks.append(lax.fori_loop(0, TAPS, place, jnp.zeros(part, F32)))
-    return chunks[0] if len(chunks) == 1 else jnp.concatenate(chunks, axis=0)
+    row = lax.broadcasted_iota(jnp.int32, (8, 256), 0)
+    col = lax.broadcasted_iota(jnp.int32, (8, 256), 1)
+    d = ((row - col if in_dim == 0 else col - row) + shift + 512) & 255
+    first = jnp.zeros((8, 256), F32)
+    for k in range(TAPS):
+        first = jnp.where(d == k, taps[level, k], first)
+    parts = [first] + [pltpu.roll(first, at, 1) for at in range(8, shape[0], 8)]
+    return jnp.concatenate([p[:, 0 : shape[1]] for p in parts], axis=0)
 
 
 def between(shape, dim, low, high):
@@ -245,6 +242,8 @@
         return send(q.at[src], q.at[dst], halo_s.at[i], halo_r.at[i], target)
 
     loads["heat"].wait()
+    q[EXT:DEEP, :] = jnp.zeros((DEEP - EXT, WIDE), F32)
+
     loads["rows"].wait()
     loads["res"].wait()
     own_h, own_l = split(q[own_rows, SIDE : SIDE + COLS])
@@ -338,7 +337,7 @@
 
     low, high = jnp.where(w == 0, HALO, 0), jnp.where(w == NW - 1, HALO + ROWS, EXT)
     t0 = jnp.where(
-        between((ROWS, EXT), 1, low, high), band((ROWS, EXT), 1, 8 - HALO, taps, 0), 0.0
+        between((ROWS, DEEP), 1, low, high), band((ROWS, DEEP), 1, 8 - HALO, taps, 0), 0.0
     )
 
     def row_level(level, size, res, pro):
@@ -346,30 +345,31 @@
         tr_h, tr_l = split(mm_left(th, tl, res))
         return mm_right(pro, tr_h, tr_l)
 
-    for i, m in enumerate(
-        (t0, row_level(1, 128, rm("r1", EXT), rm("p1", 128)), row_level(2, 64, rm("r21", EXT), rm("p12", 64)))
-    ):
+    row_maps_of = (
+        t0,
+        row_level(1, 128, rm("r1", DEEP), rm("p1", 128)),
+        row_level(2, 64, rm("r21", DEEP), rm("p12", 64)),
+    )
+    for i, m in enumerate(row_maps_of):
         hi, lo = split(m)
-        mr[i * ROWS : (i + 1) * ROWS, :] = hi
-        mr[(i + 3) * ROWS : (i + 4) * ROWS, :] = lo
+        at_i = slice(i * ROWS, (i + 1) * ROWS)
+        mr[at_i, 0:DEEP] = hi
+        mr[at_i, DEEP : 2 * DEEP] = lo
+        mr[at_i, 2 * DEEP : 3 * DEEP] = hi
+
+    fine_band = band((WIN, TILE), 0, 8 - MARGIN, taps, 0)
+    coarse_bands = [split(band((size, size), 0, 8, taps, t)) for t, size in ((1, 128), (2, 64))]
 
     def col_maps_of(i, low, high):
         def cm(name, cols):
             start, rows = COL_AT[name]
             return cmap[i, start : start + rows, 0:cols]
 
-        maps = [
-            jnp.where(
-                between((WIN, TILE), 0, low, high),
-                band((WIN, TILE), 0, 8 - MARGIN, taps, 0),
-                0.0,
-            )
-        ]
-        for level, size, res, pro in (
-            (1, 128, cm("r1", 128), cm("p1", 128)),
-            (2, 64, cm("r21", 64), cm("p12", 128)),
+        maps = [jnp.where(between((WIN, TILE), 0, low, high), fine_band, 0.0)]
+        for (th, tl), res, pro in (
+            (coarse_bands[0], cm("r1", 128), cm("p1", 128)),
+            (coarse_bands[1], cm("r21", 64), cm("p12", 128)),
         ):
-            th, tl = split(band((size, size), 0, 8, taps, level))
             tp_h, tp_l = split(mm_left(th, tl, pro))
             maps.append(mm_right(res, tp_h, tp_l))
         for t, m in enumerate(maps):
@@ -379,14 +379,12 @@
 
     loads["cols"].wait()
     loads["rim_cols"].wait()
-
-    @pl.loop(0, 2)
-    def _(i):
-        col_maps_of(
-            i,
-            jnp.where((i == 1) & (n == 0), MARGIN, 0),
-            jnp.where((i == 1) & (n == NN - 1), MARGIN + TILE, WIN),
-        )
+    col_maps_of(0, 0, WIN)
+    col_maps_of(
+        1,
+        jnp.where(n == 0, MARGIN, 0),
+        jnp.where(n == NN - 1, MARGIN + TILE, WIN),
+    )
 
     for c in plane:
         c.wait_recv()
@@ -425,12 +423,13 @@
     for c in outer:
         c.wait_recv()
 
-    @pl.loop(0, SPAN // 128)
+    @pl.loop(0, 5)
     def _(j):
-        here = q[:, pl.ds(pl.multiple_of(128 * j, 128), 256)]
-        hi, lo = split(pltpu.roll(here, 256 - MARGIN, 1)[:, 0:128])
-        res = mm_both(mr[0 : 3 * ROWS], mr[3 * ROWS :], hi, lo)
-        at_j = pl.ds(pl.multiple_of(128 * j, 128), 128)
+        start = pl.multiple_of(128 * jnp.minimum(2 * j, SPAN // 128 - 2), 128)
+        here = pltpu.roll(q[:, pl.ds(start, 384)], 384 - MARGIN, 1)[:, 0:256]
+        hi, lo = split(here)
+        res = mm(mr[...], jnp.concatenate([hi, hi, lo], axis=0))
+        at_j = pl.ds(start, 256)
         y_hl[0, :, at_j], y_hl[1, :, at_j] = split(res)
 
     for c in partial_sums:
@@ -499,7 +498,7 @@
         out_specs=far_memory,
         scratch_shapes=[
             pltpu.SMEM((3, TAPS), F32),
-            words(EXT, WIDE),
+            words(DEEP, WIDE),
             words(16, COLS),
             words(NQ, 2, 16, 128),
             words(NQ, 2, 16, 128),
@@ -511,7 +510,7 @@
             halves(*maps[2].shape[1:]),
             halves(*maps[3].shape[1:]),
             halves(*maps[4].shape),
-            halves(6 * ROWS, EXT),
+            halves(3 * ROWS, 3 * DEEP),
             halves(2, 3 * ROWS, SPAN),
             halves(144, COLS),
             halves(144, COLS),

time: 43.7 us -> 43.7 us (level)
  no operation moved by 1% of the time
where the time goes in v4:
time: 43.7 us; the launch traced here: 43.5 us
  Pallas kernels  41.6 us (95%)
  local copies, waits for them, and re-layouts  1.89 us (4%)
    pallas_call x1, Pallas kernels, shards(): pl.pallas_call(kernel, out_shape=jax.ShapeDtypeStruct((ROWS, COLS), F32),...  41.6 us
    unnamed x1, local copies, waits for them, and re-layouts  1.89 us

profile of v4, /device:TPU:1, one launch (start us, length us, event | category | flops | bytes accessed | tf_op | source)
XLA Modules:
  0.0 43.5 jit_solution(2018964018074443331)
XLA Ops:
  0.0 41.6 %shard_map.91 = f32[128,1024]{1,0:T(8,128)} custom-call(f32[128,1024]{1,0:T(8,128)} %heat.1, f32[3,17]{1,0:T(4,128)} %taps_in.1, f32[16,1024]{1,0:T(8,128)} %top_rows.1, f32[128,1024]{1,0:T(8,128)} %top_cols.1, bf16[3,608,256]{2,1,0:T(8,128)(2,1)} %constant.10.clone.row_maps, bf16[3,704,128]{2,1,0:T(8,128)(2,1)} %constant.11.clone.col_maps, ...), custom_call_target="tpu_custom_call" | custom-call | tf_op jit(solution)/shard_map/pallas_call | solution.py:494
  41.6 1.9 %copy.11 = f32[128,1024]{1,0:T(8,128)} copy(f32[128,1024]{1,0:T(8,128)} %shard_map.91) | data formatting | bytes 1048576

commit v5 on v4

--- a/solution.py
+++ b/solution.py
@@ -264,11 +264,6 @@
             send(es.at[row_part[dw], col_part[dn]], dst, rim_s.at[i], rim_r.at[i], dev(dw, dn))
         )
 
-    strips = [
-        strip((own_rows, slice(COLS, COLS + SIDE)), (own_rows, slice(0, SIDE)), 0, dev(0, 1)),
-        strip((own_rows, slice(SIDE, 2 * SIDE)), (own_rows, slice(SIDE + COLS, WIDE)), 1, dev(0, -1)),
-    ]
-
     loads["top_rows"].wait()
     loads["sort"].wait()
     halves = [split(aw[:, 512 * p : 512 * (p + 1)]) for p in range(2)]
@@ -307,18 +302,6 @@
         for p in range(NQ):
             rim_up(p).start()
 
-    loads["top_cols"].wait()
-    sides = [
-        send(bx.at[128:136], bx.at[0:8], bx_s.at[0], bx_r.at[0], dev(0, 1)),
-        send(bx.at[8:16], bx.at[136:144], bx_s.at[1], bx_r.at[1], dev(0, -1)),
-    ]
-    for c in strips:
-        c.wait_recv()
-    outer = [
-        strip(slice(ROWS, ROWS + HALO), slice(0, HALO), 2, dev(1, 0)),
-        strip(slice(HALO, 2 * HALO), slice(HALO + ROWS, EXT), 3, dev(-1, 0)),
-    ]
-
     for c in rims:
         c.wait_recv()
     mid = nb_mid[0] + nb_mid[1]
@@ -331,6 +314,16 @@
 
     column = [
         send(g.at[z], g.at[z], z_s.at[i], z_r.at[i], in_z(dz)) for i, dz in enumerate(along)
+    ]
+
+    strips = [
+        strip((own_rows, slice(COLS, COLS + SIDE)), (own_rows, slice(0, SIDE)), 0, dev(0, 1)),
+        strip((own_rows, slice(SIDE, 2 * SIDE)), (own_rows, slice(SIDE + COLS, WIDE)), 1, dev(0, -1)),
+    ]
+    loads["top_cols"].wait()
+    sides = [
+        send(bx.at[128:136], bx.at[0:8], bx_s.at[0], bx_r.at[0], dev(0, 1)),
+        send(bx.at[8:16], bx.at[136:144], bx_s.at[1], bx_r.at[1], dev(0, -1)),
     ]
 
     loads["taps"].wait()
@@ -356,6 +349,13 @@
         mr[at_i, 0:DEEP] = hi
         mr[at_i, DEEP : 2 * DEEP] = lo
         mr[at_i, 2 * DEEP : 3 * DEEP] = hi
+
+    for c in strips:
+        c.wait_recv()
+    outer = [
+        strip(slice(ROWS, ROWS + HALO), slice(0, HALO), 2, dev(1, 0)),
+        strip(slice(HALO, 2 * HALO), slice(HALO + ROWS, EXT), 3, dev(-1, 0)),
+    ]
 
     fine_band = band((WIN, TILE), 0, 8 - MARGIN, taps, 0)
     coarse_bands = [split(band((size, size), 0, 8, taps, t)) for t, size in ((1, 128), (2, 64))]
@@ -391,10 +391,11 @@
     for side, dst in ((0, at), (1, ab)):
         rim_copy(dst, dst, side, 0, 1).wait_recv()
     blocks = [at] + [ar.at[k] for k in range(NQ)] + [ab]
+    plane_rows = jnp.concatenate(
+        [jnp.concatenate([b[0], b[1]], axis=1) for b in blocks], axis=0
+    )
     a_h, a_l = split(
-        jnp.concatenate(
-            [jnp.concatenate([b[0], b[1]], axis=1) for b in blocks], axis=0
-        )
+        jnp.concatenate([plane_rows[16 * k + 7 : 16 * k + 31] for k in range(NQ)], axis=0)
     )
     for c in sides:
         c.wait_recv()
@@ -409,16 +410,14 @@
     for c in column:
         c.wait_recv()
     g_h, g_l = split(g[...].reshape(256, 128))
-    ps[...] = mm_both(a_h, a_l, g_h, g_l)
+    ps[...] = mm_both(a_h, a_l, g_h, g_l).reshape(NQ, 24, 128)
 
     partial_sums = []
     for i, (k, dx) in enumerate(hops):
-        start = pl.multiple_of(16 * ((qi + k) % NQ), 16)
         partial_sums.append(
-            send(ps.at[pl.ds(start, 32)], pa.at[xl, k], pa_s.at[i], pa_r.at[i], in_row(k, dx))
-        )
-    own = pl.multiple_of(16 * qi, 16)
-    pa[xl, 0] = ps[pl.ds(own, 32), :]
+            send(ps.at[(qi + k) % NQ], pa.at[xl, k], pa_s.at[i], pa_r.at[i], in_row(k, dx))
+        )
+    pa[xl, 0] = ps[qi]
 
     for c in outer:
         c.wait_recv()
@@ -436,7 +435,7 @@
         c.wait_recv()
     for b in range(2):
         total = (pa[b, 0] + pa[b, 1]) + (pa[b, 2] + pa[b, 3])
-        xb[y, :, 128 * b : 128 * (b + 1)] = total[7:31, :]
+        xb[y, :, 128 * b : 128 * (b + 1)] = total
     lines = [
         send(xb.at[y], xb.at[y], xb_s.at[k - 1], xb_r.at[k - 1], in_y(k)) for k in range(1, NY)
     ]
@@ -519,8 +518,8 @@
             words(8, 8, 128),
             words(2, 16, 128),
             words(NZ, 16, 128),
-            words(80, 128),
-            words(2, NQ, 32, 128),
+            words(NQ, 24, 128),
+            words(2, NQ, 24, 128),
             words(NY, 24, 256),
             words(ROWS, COLS),
         ]

time: 43.7 us -> 45.2 us (1.034)
  Pallas kernels: 41.6 us -> 43.1 us
    pallas_call x1, Pallas kernels: 41.6 us -> 43.1 us  [shards(): pl.pallas_call(kernel, out_shape=jax.ShapeDtypeStruct((ROWS, COLS), F32),...]
where the time goes in v5:
time: 45.2 us; the launch traced here: 45 us
  Pallas kernels  43.1 us (95%)
  local copies, waits for them, and re-layouts  1.89 us (4%)
    pallas_call x1, Pallas kernels, shards(): pl.pallas_call(kernel, out_shape=jax.ShapeDtypeStruct((ROWS, COLS), F32),...  43.1 us
    unnamed x1, local copies, waits for them, and re-layouts  1.89 us

profile of v5, /device:TPU:1, one launch (start us, length us, event | category | flops | bytes accessed | tf_op | source)
XLA Modules:
  0.0 45.0 jit_solution(6546127517885970698)
XLA Ops:
  0.0 43.1 %shard_map.91 = f32[128,1024]{1,0:T(8,128)} custom-call(f32[128,1024]{1,0:T(8,128)} %heat.1, f32[3,17]{1,0:T(4,128)} %taps_in.1, f32[16,1024]{1,0:T(8,128)} %top_rows.1, f32[128,1024]{1,0:T(8,128)} %top_cols.1, bf16[3,608,256]{2,1,0:T(8,128)(2,1)} %constant.10.clone.row_maps, bf16[3,704,128]{2,1,0:T(8,128)(2,1)} %constant.11.clone.col_maps, ...), custom_call_target="tpu_custom_call" | custom-call | tf_op jit(solution)/shard_map/pallas_call | solution.py:493
  43.1 1.9 %copy.11 = f32[128,1024]{1,0:T(8,128)} copy(f32[128,1024]{1,0:T(8,128)} %shard_map.91) | data formatting | bytes 1048576

commit v6 on v5

--- a/solution.py
+++ b/solution.py
@@ -165,27 +165,30 @@
 
 
 def kernel(
-    heat, taps_in, top_rows, top_cols, row_maps, col_maps, col_res, col_top, sort, out,
+    heat, taps_in, top_rows, top_cols, row_maps, col_maps, col_res, col_top, sort, near_out, top_out, row_out,
     taps, q, aw, to, ar, at, ab, bx, rmap, cmap, cres, ctop, perm,
-    mr, y_hl, b_h, b_l, cm_w, es, nb, nb_mid, g, ps, pa, xb, acc,
+    mr, y_hl, b_h, b_l, cm_w, es, nb, nb_mid, g, ps, pa, xb, acc, top_f, top_u,
     load_sem, rim_s, rim_r, halo_s, halo_r, aa_s, aa_r, ah_s, ah_r, bx_s, bx_r,
     z_s, z_r, pa_s, pa_r, xb_s, xb_r, out_s,
 ):
     w, n = lax.axis_index("wide"), lax.axis_index("narrow")
-    z, qi = w // NQ, w % NQ
-    y, xl = n // 2, n % 2
+    rem = lax.rem
+    z, qi = lax.div(w, NQ), rem(w, NQ)
+    y, xl = lax.div(n, 2), rem(n, 2)
+    row_at = z * NQ
+    pair_at = n - xl
 
     def dev(dw, dn):
-        return ((w + dw + NW) % NW, (n + dn + NN) % NN)
+        return (rem(w + (dw + NW), NW) if dw else w, rem(n + (dn + NN), NN) if dn else n)
 
     def in_z(dz):
-        return (((z + dz + NZ) % NZ) * NQ + qi, n)
+        return (rem(w + (dz + NZ) * NQ, NW), n)
 
     def in_row(k, dx):
-        return (z * NQ + (qi + k + NQ) % NQ, 2 * y + (xl + dx) % 2)
+        return (row_at + rem(qi + (k + NQ), NQ) if k else w, pair_at + 1 - xl if dx else n)
 
     def in_y(dy):
-        return (w, 2 * ((y + dy + NY) % NY) + xl)
+        return (w, rem(n + 2 * dy, NN))
 
     row_v = jnp.where(w == 0, 0, jnp.where(w == NW - 1, 2, 1))
     col_v = jnp.where(n == 0, 0, jnp.where(n == NN - 1, 2, 1))
@@ -218,7 +221,7 @@
     along = [8] + [d for dz in range(7, 0, -1) for d in (dz, -dz)]
     greet += [in_z(dz) for dz in along]
     count = len(greet)
-    greet += [(((z + NZ - 1) % NZ) * NQ + NQ - 1, n), (((z + 1) % NZ) * NQ, n)]
+    greet += [(rem(row_at + (NW - 1), NW), n), (rem(row_at + NQ, NW), n)]
     for target in greet:
         pl.semaphore_signal(barrier, inc=1, device_id=target, device_id_type=MESH)
     for name in ("top_rows", "sort", "top_cols", "taps", "cols", "rim_cols", "top"):
@@ -264,6 +267,11 @@
             send(es.at[row_part[dw], col_part[dn]], dst, rim_s.at[i], rim_r.at[i], dev(dw, dn))
         )
 
+    strips = [
+        strip((own_rows, slice(COLS, COLS + SIDE)), (own_rows, slice(0, SIDE)), 0, dev(0, 1)),
+        strip((own_rows, slice(SIDE, 2 * SIDE)), (own_rows, slice(SIDE + COLS, WIDE)), 1, dev(0, -1)),
+    ]
+
     loads["top_rows"].wait()
     loads["sort"].wait()
     halves = [split(aw[:, 512 * p : 512 * (p + 1)]) for p in range(2)]
@@ -275,7 +283,7 @@
         for k in range(NQ):
             to[k, p] = sorted_cols[16 * p : 16 * (p + 1), 128 * k : 128 * (k + 1)]
     plane = [
-        send(to.at[(qi + k) % NQ], ar.at[qi], aa_s.at[k - 1], aa_r.at[k - 1], in_row(k, 0))
+        send(to.at[rem(qi + k, NQ)], ar.at[qi], aa_s.at[k - 1], aa_r.at[k - 1], in_row(k, 0))
         for k in (1, 2, 3)
     ]
     ar[qi] = to[qi]
@@ -283,7 +291,7 @@
     def rim_copy(src, dst, side, p, dz):
         return pltpu.make_async_remote_copy(
             src_ref=src, dst_ref=dst, send_sem=ah_s.at[p], recv_sem=ah_r.at[side],
-            device_id=(((z + dz + NZ) % NZ) * NQ + p, n), device_id_type=MESH,
+            device_id=(rem(row_at + ((dz + NZ) * NQ + p), NW), n), device_id_type=MESH,
         )
 
     def rim_down(p):
@@ -316,10 +324,13 @@
         send(g.at[z], g.at[z], z_s.at[i], z_r.at[i], in_z(dz)) for i, dz in enumerate(along)
     ]
 
-    strips = [
-        strip((own_rows, slice(COLS, COLS + SIDE)), (own_rows, slice(0, SIDE)), 0, dev(0, 1)),
-        strip((own_rows, slice(SIDE, 2 * SIDE)), (own_rows, slice(SIDE + COLS, WIDE)), 1, dev(0, -1)),
-    ]
+    for c in strips:
+        c.wait_recv()
+    outer = [
+        strip(slice(ROWS, ROWS + HALO), slice(0, HALO), 2, dev(1, 0)),
+        strip(slice(HALO, 2 * HALO), slice(HALO + ROWS, EXT), 3, dev(-1, 0)),
+    ]
+
     loads["top_cols"].wait()
     sides = [
         send(bx.at[128:136], bx.at[0:8], bx_s.at[0], bx_r.at[0], dev(0, 1)),
@@ -349,13 +360,6 @@
         mr[at_i, 0:DEEP] = hi
         mr[at_i, DEEP : 2 * DEEP] = lo
         mr[at_i, 2 * DEEP : 3 * DEEP] = hi
-
-    for c in strips:
-        c.wait_recv()
-    outer = [
-        strip(slice(ROWS, ROWS + HALO), slice(0, HALO), 2, dev(1, 0)),
-        strip(slice(HALO, 2 * HALO), slice(HALO + ROWS, EXT), 3, dev(-1, 0)),
-    ]
 
     fine_band = band((WIN, TILE), 0, 8 - MARGIN, taps, 0)
     coarse_bands = [split(band((size, size), 0, 8, taps, t)) for t, size in ((1, 128), (2, 64))]
@@ -407,17 +411,8 @@
 
     loads["top"].wait()
 
-    for c in column:
-        c.wait_recv()
-    g_h, g_l = split(g[...].reshape(256, 128))
-    ps[...] = mm_both(a_h, a_l, g_h, g_l).reshape(NQ, 24, 128)
-
-    partial_sums = []
-    for i, (k, dx) in enumerate(hops):
-        partial_sums.append(
-            send(ps.at[(qi + k) % NQ], pa.at[xl, k], pa_s.at[i], pa_r.at[i], in_row(k, dx))
-        )
-    pa[xl, 0] = ps[qi]
+    top_u[:, 0:32] = rm("top", 32)
+    top_u[:, 32:64] = rm("top", 32)
 
     for c in outer:
         c.wait_recv()
@@ -430,15 +425,6 @@
         res = mm(mr[...], jnp.concatenate([hi, hi, lo], axis=0))
         at_j = pl.ds(start, 256)
         y_hl[0, :, at_j], y_hl[1, :, at_j] = split(res)
-
-    for c in partial_sums:
-        c.wait_recv()
-    for b in range(2):
-        total = (pa[b, 0] + pa[b, 1]) + (pa[b, 2] + pa[b, 3])
-        xb[y, :, 128 * b : 128 * (b + 1)] = total
-    lines = [
-        send(xb.at[y], xb.at[y], xb_s.at[k - 1], xb_r.at[k - 1], in_y(k)) for k in range(1, NY)
-    ]
 
     @pl.loop(0, TILES)
     def _(j):
@@ -453,6 +439,34 @@
             both[0:ROWS, TILE:] + both[ROWS:, 0:TILE]
         )
 
+    results = [
+        pltpu.make_async_copy(acc, near_out, out_s.at[0]),
+        pltpu.make_async_copy(top_u, row_out, out_s.at[1]),
+    ]
+    for c in results:
+        c.start()
+
+    for c in column:
+        c.wait_recv()
+    g_h, g_l = split(g[...].reshape(256, 128))
+    ps[...] = mm_both(a_h, a_l, g_h, g_l).reshape(NQ, 24, 128)
+
+    partial_sums = []
+    for i, (k, dx) in enumerate(hops):
+        partial_sums.append(
+            send(ps.at[rem(qi + k, NQ)], pa.at[xl, k], pa_s.at[i], pa_r.at[i], in_row(k, dx))
+        )
+    pa[xl, 0] = ps[qi]
+
+    for c in partial_sums:
+        c.wait_recv()
+    for b in range(2):
+        total = (pa[b, 0] + pa[b, 1]) + (pa[b, 2] + pa[b, 3])
+        xb[y, :, 128 * b : 128 * (b + 1)] = total
+    lines = [
+        send(xb.at[y], xb.at[y], xb_s.at[k - 1], xb_r.at[k - 1], in_y(k)) for k in range(1, NY)
+    ]
+
     for c in lines:
         c.wait_recv()
     lines_in = jnp.concatenate([xb[i] for i in range(NY)], axis=1)
@@ -460,13 +474,10 @@
     with_hi = mm_nt(jnp.concatenate([x_h, x_l], axis=0), b_h[...])
     e_h, e_l = split(with_hi[0:32] + (with_hi[32:64] + mm_nt(x_h, b_l[...])))
     f_h, f_l = split(mm_left(e_h, e_l, ctop[...]))
-    ur = rm("top", 32)
-    pieces = []
-    for i in range(4):
-        at_i = slice(256 * i, 256 * (i + 1))
-        acc[:, at_i] += mm_right(ur, f_h[:, at_i], f_l[:, at_i])
-        pieces.append(pltpu.make_async_copy(acc.at[:, at_i], out.at[:, at_i], out_s.at[i]))
-        pieces[-1].start()
+    top_f[0:32, :] = f_h
+    top_f[32:64, :] = f_l
+    results.append(pltpu.make_async_copy(top_f, top_out, out_s.at[2]))
+    results[-1].start()
 
     for c in rims + strips + plane + sides + outer + column + partial_sums + lines:
         c.wait_send()
@@ -481,20 +492,24 @@
         for p in range(NQ):
             rim_up(p).wait_send()
 
-    for c in pieces:
+    for c in results:
         c.wait()
 
 
 def shards(maps, heat_power, level_taps, top_rows, top_cols):
     far_memory = pl.BlockSpec(memory_space=pltpu.HBM)
-    sems = [10, 8, 8, 4, 4, 3, 3, 4, 2, 2, 2, 15, 15, 7, 7, 3, 3, 4]
+    sems = [10, 8, 8, 4, 4, 3, 3, 4, 2, 2, 2, 15, 15, 7, 7, 3, 3, 3]
     words = lambda *shape: pltpu.VMEM(shape, F32)
     halves = lambda *shape: pltpu.VMEM(shape, BF16)
-    return pl.pallas_call(
+    near, top, row = pl.pallas_call(
         kernel,
-        out_shape=jax.ShapeDtypeStruct((ROWS, COLS), F32),
+        out_shape=[
+            jax.ShapeDtypeStruct((ROWS, COLS), F32),
+            jax.ShapeDtypeStruct((64, COLS), BF16),
+            jax.ShapeDtypeStruct((ROWS, 64), BF16),
+        ],
         in_specs=[far_memory] * (4 + len(maps)),
-        out_specs=far_memory,
+        out_specs=[far_memory] * 3,
         scratch_shapes=[
             pltpu.SMEM((3, TAPS), F32),
             words(DEEP, WIDE),
@@ -522,12 +537,15 @@
             words(2, NQ, 24, 128),
             words(NY, 24, 256),
             words(ROWS, COLS),
+            halves(64, COLS),
+            halves(ROWS, 64),
         ]
         + [pltpu.SemaphoreType.DMA((k,)) for k in sems],
         compiler_params=pltpu.CompilerParams(
             collective_id=0, has_side_effects=True, vmem_limit_bytes=62 * 1024 * 1024
         ),
     )(heat_power, level_taps, top_rows, top_cols, *maps)
+    return near + mm(row, top)
 
 
 def solution(mesh):

time: 45.2 us -> 47.5 us (1.051)
  matrix products: 0 us -> 2.14 us
  Pallas kernels: 43.1 us -> 45.2 us
  local copies, waits for them, and re-layouts: 1.89 us -> 0 us
    dot_general x0 -> x1, matrix products: none -> 2.14 us  [mm(): return jnp.dot(a, b, preferred_element_type=F32)]
    pallas_call x1, Pallas kernels: 43.1 us -> 45.2 us  [shards(): pl.pallas_call(kernel, out_shape=[jax.ShapeDtypeStruct((ROWS, COLS), F32)...]
    unnamed x1 -> x0, local copies, waits for them, and re-layouts: 1.89 us -> none
where the time goes in v6:
time: 47.5 us; the launch traced here: 47.4 us
  Pallas kernels  45.2 us (95%)
  matrix products  2.14 us (5%)
    pallas_call x1, Pallas kernels, shards(): pl.pallas_call(kernel, out_shape=[jax.ShapeDtypeStruct((ROWS, COLS), F32)...  45.2 us
    dot_general x1, matrix products, mm(): return jnp.dot(a, b, preferred_element_type=F32)  2.14 us

profile of v6, /device:TPU:1, one launch (start us, length us, event | category | flops | bytes accessed | tf_op | source)
XLA Modules:
  0.0 47.4 jit_solution(6750245806660823206)
XLA Ops:
  0.0 45.2 %shard_map.91 = (f32[128,1024]{1,0:T(8,128)}, bf16[64,1024]{1,0:T(8,128)(2,1)}, bf16[128,64]{1,0:T(8,128)(2,1)}) custom-call(f32[128,1024]{1,0:T(8,128)} %heat.1, f32[3,17]{1,0:T(4,128)} %taps_in.1, f32[16,1024]{1,0:T(8,128)} %top_rows.1, f32[128,1024]{1,0:T(8,128)} %top_cols.1, bf16[3,608,256]{2,1,0:T(8,128)(2,1)} %constant.10.clone.row_maps, ...), custom_call_target="tpu_custom_call" | custom-call | tf_op jit(solution)/shard_map/pallas_call | solution.py:504
  45.2 2.1 %convolution_add_fusion = f32[128,1024]{1,0:T(8,128)} fusion(f32[128,1024]{1,0:T(8,128)} %get-tuple-element.8, bf16[128,64]{1,0:T(8,128)(2,1)} %get-tuple-element.9, bf16[64,1024]{1,0:T(8,128)(2,1)} %get-tuple-element.10), kind=kOutput, calls=%fused_computation | convolution fusion | flops 16908288 | bytes 1196032 | tf_op jit(solution)/shard_map/dot_general | solution.py:129

commit v7 on v6

--- a/solution.py
+++ b/solution.py
@@ -310,6 +310,19 @@
         for p in range(NQ):
             rim_up(p).start()
 
+    loads["top_cols"].wait()
+    sides = [
+        send(bx.at[128:136], bx.at[0:8], bx_s.at[0], bx_r.at[0], dev(0, 1)),
+        send(bx.at[8:16], bx.at[136:144], bx_s.at[1], bx_r.at[1], dev(0, -1)),
+    ]
+
+    for c in strips:
+        c.wait_recv()
+    outer = [
+        strip(slice(ROWS, ROWS + HALO), slice(0, HALO), 2, dev(1, 0)),
+        strip(slice(HALO, 2 * HALO), slice(HALO + ROWS, EXT), 3, dev(-1, 0)),
+    ]
+
     for c in rims:
         c.wait_recv()
     mid = nb_mid[0] + nb_mid[1]
@@ -322,19 +335,6 @@
 
     column = [
         send(g.at[z], g.at[z], z_s.at[i], z_r.at[i], in_z(dz)) for i, dz in enumerate(along)
-    ]
-
-    for c in strips:
-        c.wait_recv()
-    outer = [
-        strip(slice(ROWS, ROWS + HALO), slice(0, HALO), 2, dev(1, 0)),
-        strip(slice(HALO, 2 * HALO), slice(HALO + ROWS, EXT), 3, dev(-1, 0)),
-    ]
-
-    loads["top_cols"].wait()
-    sides = [
-        send(bx.at[128:136], bx.at[0:8], bx_s.at[0], bx_r.at[0], dev(0, 1)),
-        send(bx.at[8:16], bx.at[136:144], bx_s.at[1], bx_r.at[1], dev(0, -1)),
     ]
 
     loads["taps"].wait()
@@ -411,6 +411,18 @@
 
     loads["top"].wait()
 
+    for c in column:
+        c.wait_recv()
+    g_h, g_l = split(g[...].reshape(256, 128))
+    ps[...] = mm_both(a_h, a_l, g_h, g_l).reshape(NQ, 24, 128)
+
+    partial_sums = []
+    for i, (k, dx) in enumerate(hops):
+        partial_sums.append(
+            send(ps.at[rem(qi + k, NQ)], pa.at[xl, k], pa_s.at[i], pa_r.at[i], in_row(k, dx))
+        )
+    pa[xl, 0] = ps[qi]
+
     top_u[:, 0:32] = rm("top", 32)
     top_u[:, 32:64] = rm("top", 32)
 
@@ -425,6 +437,15 @@
         res = mm(mr[...], jnp.concatenate([hi, hi, lo], axis=0))
         at_j = pl.ds(start, 256)
         y_hl[0, :, at_j], y_hl[1, :, at_j] = split(res)
+
+    for c in partial_sums:
+        c.wait_recv()
+    for b in range(2):
+        total = (pa[b, 0] + pa[b, 1]) + (pa[b, 2] + pa[b, 3])
+        xb[y, :, 128 * b : 128 * (b + 1)] = total
+    lines = [
+        send(xb.at[y], xb.at[y], xb_s.at[k - 1], xb_r.at[k - 1], in_y(k)) for k in range(1, NY)
+    ]
 
     @pl.loop(0, TILES)
     def _(j):
@@ -445,27 +466,6 @@
     ]
     for c in results:
         c.start()
-
-    for c in column:
-        c.wait_recv()
-    g_h, g_l = split(g[...].reshape(256, 128))
-    ps[...] = mm_both(a_h, a_l, g_h, g_l).reshape(NQ, 24, 128)
-
-    partial_sums = []
-    for i, (k, dx) in enumerate(hops):
-        partial_sums.append(
-            send(ps.at[rem(qi + k, NQ)], pa.at[xl, k], pa_s.at[i], pa_r.at[i], in_row(k, dx))
-        )
-    pa[xl, 0] = ps[qi]
-
-    for c in partial_sums:
-        c.wait_recv()
-    for b in range(2):
-        total = (pa[b, 0] + pa[b, 1]) + (pa[b, 2] + pa[b, 3])
-        xb[y, :, 128 * b : 128 * (b + 1)] = total
-    lines = [
-        send(xb.at[y], xb.at[y], xb_s.at[k - 1], xb_r.at[k - 1], in_y(k)) for k in range(1, NY)
-    ]
 
     for c in lines:
         c.wait_recv()

time: 47.5 us -> 43.4 us (0.914)
  Pallas kernels: 45.2 us -> 41.1 us
    pallas_call x1, Pallas kernels: 45.2 us -> 41.1 us  [shards(): pl.pallas_call(kernel, out_shape=[jax.ShapeDtypeStruct((ROWS, COLS), F32)...]
where the time goes in v7:
time: 43.4 us; the launch traced here: 43.3 us
  Pallas kernels  41.1 us (95%)
  matrix products  2.14 us (5%)
    pallas_call x1, Pallas kernels, shards(): pl.pallas_call(kernel, out_shape=[jax.ShapeDtypeStruct((ROWS, COLS), F32)...  41.1 us
    dot_general x1, matrix products, mm(): return jnp.dot(a, b, preferred_element_type=F32)  2.14 us

profile of v7, /device:TPU:1, one launch (start us, length us, event | category | flops | bytes accessed | tf_op | source)
XLA Modules:
  0.0 43.3 jit_solution(12608029258758573980)
XLA Ops:
  0.0 41.1 %shard_map.91 = (f32[128,1024]{1,0:T(8,128)}, bf16[64,1024]{1,0:T(8,128)(2,1)}, bf16[128,64]{1,0:T(8,128)(2,1)}) custom-call(f32[128,1024]{1,0:T(8,128)} %heat.1, f32[3,17]{1,0:T(4,128)} %taps_in.1, f32[16,1024]{1,0:T(8,128)} %top_rows.1, f32[128,1024]{1,0:T(8,128)} %top_cols.1, bf16[3,608,256]{2,1,0:T(8,128)(2,1)} %constant.10.clone.row_maps, ...), custom_call_target="tpu_custom_call" | custom-call | tf_op jit(solution)/shard_map/pallas_call | solution.py:504
  41.1 2.1 %convolution_add_fusion = f32[128,1024]{1,0:T(8,128)} fusion(f32[128,1024]{1,0:T(8,128)} %get-tuple-element.8, bf16[128,64]{1,0:T(8,128)(2,1)} %get-tuple-element.9, bf16[64,1024]{1,0:T(8,128)(2,1)} %get-tuple-element.10), kind=kOutput, calls=%fused_computation | convolution fusion | flops 16908288 | bytes 1196032 | tf_op jit(solution)/shard_map/dot_general | solution.py:129

commit v8 on v7

--- a/solution.py
+++ b/solution.py
@@ -100,7 +100,7 @@
                     padded(own_to_top(ROWS, v), 32, 256),
                     padded(r1, 128, 256),
                     padded(r2 @ r1, 64, 256),
-                    padded(p1, 128, 256),
+                    padded(np.concatenate([p1[:, 12:92], (p1 @ p2)[:, 2:50]], 1), 128, 256),
                     padded(p1 @ p2, 128, 256),
                     padded(top_prolong(ROWS, 24, -1, v), 128, 256),
                 ]
@@ -344,22 +344,22 @@
         between((ROWS, DEEP), 1, low, high), band((ROWS, DEEP), 1, 8 - HALO, taps, 0), 0.0
     )
 
-    def row_level(level, size, res, pro):
-        th, tl = split(band((size, size), 1, 8, taps, level))
-        tr_h, tr_l = split(mm_left(th, tl, res))
-        return mm_right(pro, tr_h, tr_l)
-
-    row_maps_of = (
-        t0,
-        row_level(1, 128, rm("r1", DEEP), rm("p1", 128)),
-        row_level(2, 64, rm("r21", DEEP), rm("p12", 64)),
-    )
-    for i, m in enumerate(row_maps_of):
-        hi, lo = split(m)
-        at_i = slice(i * ROWS, (i + 1) * ROWS)
-        mr[at_i, 0:DEEP] = hi
-        mr[at_i, DEEP : 2 * DEEP] = lo
-        mr[at_i, 2 * DEEP : 3 * DEEP] = hi
+    def row_level(level, shape, shift, res):
+        th, tl = split(band(shape, 1, shift, taps, level))
+        return mm_left(th, tl, res)
+
+    row_maps_of = jnp.concatenate(
+        [
+            t0,
+            row_level(1, (80, 128), -4, rm("r1", DEEP)),
+            row_level(2, (48, 64), 6, rm("r21", DEEP)),
+        ],
+        axis=0,
+    )
+    hi, lo = split(row_maps_of)
+    mr[:, 0:DEEP] = hi
+    mr[:, DEEP : 2 * DEEP] = lo
+    mr[:, 2 * DEEP : 3 * DEEP] = hi
 
     fine_band = band((WIN, TILE), 0, 8 - MARGIN, taps, 0)
     coarse_bands = [split(band((size, size), 0, 8, taps, t)) for t, size in ((1, 128), (2, 64))]
@@ -451,13 +451,18 @@
     def _(j):
         at_rim = ((j == 0) & (n == 0)) | ((j == TILES - 1) & (n == NN - 1))
         at_j = pl.ds(pl.multiple_of(TILE * j, TILE), WIN)
-        windows = [
-            jnp.concatenate([y_hl[p, t * ROWS : (t + 1) * ROWS, at_j] for t in range(3)], axis=1)
-            for p in range(2)
-        ]
-        both = mm(jnp.concatenate(windows, axis=0), cm_w[jnp.where(at_rim, 1, 0)])
-        acc[:, pl.ds(pl.multiple_of(TILE * j, TILE), TILE)] = both[0:ROWS, 0:TILE] + (
-            both[0:ROWS, TILE:] + both[ROWS:, 0:TILE]
+        which = jnp.where(at_rim, 1, 0)
+        levels = []
+        for t, (low, high) in enumerate(((0, 128), (128, 208), (208, 256))):
+            m = high - low
+            both = mm(
+                jnp.concatenate([y_hl[0, low:high, at_j], y_hl[1, low:high, at_j]], axis=0),
+                cm_w[which, WIN * t : WIN * (t + 1)],
+            )
+            levels.append(both[0:m, 0:TILE] + (both[0:m, TILE:] + both[m:, 0:TILE]))
+        z_h, z_l = split(jnp.concatenate(levels[1:], axis=0))
+        acc[:, pl.ds(pl.multiple_of(TILE * j, TILE), TILE)] = levels[0] + mm_right(
+            rm("p1", 128), z_h, z_l
         )
 
     results = [
@@ -524,8 +529,8 @@
             halves(*maps[2].shape[1:]),
             halves(*maps[3].shape[1:]),
             halves(*maps[4].shape),
-            halves(3 * ROWS, 3 * DEEP),
-            halves(2, 3 * ROWS, SPAN),
+            halves(2 * ROWS, 3 * DEEP),
+            halves(2, 2 * ROWS, SPAN),
             halves(144, COLS),
             halves(144, COLS),
             halves(2, 3 * WIN, 2 * TILE),

time: 43.4 us -> 43.4 us (level)
  no operation moved by 1% of the time
where the time goes in v8:
time: 43.4 us; the launch traced here: 43.3 us
  Pallas kernels  41.1 us (95%)
  matrix products  2.14 us (5%)
    pallas_call x1, Pallas kernels, shards(): pl.pallas_call(kernel, out_shape=[jax.ShapeDtypeStruct((ROWS, COLS), F32)...  41.1 us
    dot_general x1, matrix products, mm(): return jnp.dot(a, b, preferred_element_type=F32)  2.14 us

profile of v8, /device:TPU:1, one launch (start us, length us, event | category | flops | bytes accessed | tf_op | source)
XLA Modules:
  0.0 43.3 jit_solution(16149539335283284947)
XLA Ops:
  0.0 41.1 %shard_map.91 = (f32[128,1024]{1,0:T(8,128)}, bf16[64,1024]{1,0:T(8,128)(2,1)}, bf16[128,64]{1,0:T(8,128)(2,1)}) custom-call(f32[128,1024]{1,0:T(8,128)} %heat.1, f32[3,17]{1,0:T(4,128)} %taps_in.1, f32[16,1024]{1,0:T(8,128)} %top_rows.1, f32[128,1024]{1,0:T(8,128)} %top_cols.1, bf16[3,608,256]{2,1,0:T(8,128)(2,1)} %constant.10.clone.row_maps, ...), custom_call_target="tpu_custom_call" | custom-call | tf_op jit(solution)/shard_map/pallas_call | solution.py:509
  41.1 2.1 %convolution_add_fusion = f32[128,1024]{1,0:T(8,128)} fusion(f32[128,1024]{1,0:T(8,128)} %get-tuple-element.8, bf16[128,64]{1,0:T(8,128)(2,1)} %get-tuple-element.9, bf16[64,1024]{1,0:T(8,128)(2,1)} %get-tuple-element.10), kind=kOutput, calls=%fused_computation | convolution fusion | flops 16908288 | bytes 1196032 | tf_op jit(solution)/shard_map/dot_general | solution.py:129
